TPU v7x, 512 devices: a whole 4x8x8 slice. The times are simulated.
512 devices in a mesh: src: 32 (over x, z), tgt: 16 (over y, core).
Axes of the slice: x: 4, y: 8, z: 8, core: 2. Of those that a mesh axis runs over, the one named last changes fastest.
Arguments:
- sources: bfloat16 [262144, 64], P(('src', 'tgt')), may hold values from -2.09375 to 2.09375
- targets: bfloat16 [262144, 64], P('tgt'), may hold values from -2.09375 to 2.09375
- potential: float32 [262144], P('src'), may hold values from -1 to 112
- block_map: int32 [1024, 20], P('src'), may hold values from -1 to 1023, as said below
- counts: int32 [1024], P('src'), may hold values from 10 to 20, as said below
- step_history: float32 [8, 262144], P(None, ('src', 'tgt')), may hold values from -13 to 13
- slope_history: float32 [8, 262144], P(None, ('src', 'tgt')), may hold values from -64 to 64, as said below
Outputs:
- gradient: float32 [262144], P(('src', 'tgt'))
- direction: float32 [262144], P(('src', 'tgt'))
- target_potential: float32 [262144], P('tgt')
Inputs may be any that keep to these rules, and one draw needn't show every extreme that they name: `block_map`: row b lists counts[b] different target block numbers in slots 0 to counts[b] - 1 and -1 in the other slots; every target block is listed in some row. `counts`: some source block lists exactly 20 target blocks in every draw. For every k the sum over all points of step_history[k] slope_history[k] is positive.
All inputs are finite; a program needn't handle non-finite values.
Results may differ from a plain program's by a relative error of at most 0.0008.
Values may be sent and summed in bfloat16 or wider, within the bound.
No kernel may reach another device: no remote copies, remote signals or barrier semaphores. Data moves between devices by JAX's collectives and lax.ppermute only.
A program may use at most 64 MiB of HBM per device.

v0:
```python
import functools

import jax
import jax.numpy as jnp
from jax import lax
from jax.experimental import pallas as pl
from jax.experimental.pallas import tpu as pltpu
from jax.sharding import Mesh
from jax.sharding import PartitionSpec as P

BLOCK = 256
HALF = 128
TGT = ("tgt_0", "tgt_1")
SRC = ("src_0", "src_1")
SRC_TGT = ("src_0", "src_1", "tgt_0", "tgt_1")
NEG = -1e30
LOG2E = 1.4426950408889634
LN2 = 0.6931471805599453
entropy = 0.5
SCALE = LOG2E / entropy
UNROLL = 2
F32 = jnp.float32

VMEM = pl.BlockSpec(memory_space=pltpu.VMEM)
SMEM = pl.BlockSpec(memory_space=pltpu.SMEM)


def call(body, out_shape, ins, outs, scratch=(), cost=None):
    return pl.pallas_call(
        body,
        out_shape=out_shape,
        in_specs=ins,
        out_specs=outs,
        scratch_shapes=list(scratch),
        cost_estimate=cost,
        compiler_params=pltpu.CompilerParams(vmem_limit_bytes=40 * 2**20),
    )


def sds(shape, dtype=F32):
    return jax.ShapeDtypeStruct(shape, dtype)


def nt(a, b, precision=None):
    return lax.dot_general(
        a, b, (((1,), (1,)), ((), ())), precision=precision, preferred_element_type=F32
    )


def swap(x, axis):
    return lax.all_to_all(x, axis, 0, 0, tiled=True)


def share(x, axis):
    return swap(jnp.broadcast_to(x[None], (lax.axis_size(axis), *x.shape)), axis)


def listing_kernel(blocks, own_blocks, rank, block_map, counts, src, tgt, total):
    first = rank[0] * own_blocks

    def of_block(b, n):
        def of_slot(k, n):
            local = block_map[b, k] - first
            src[n] = b
            tgt[n] = local
            mine = (local >= 0) & (local < own_blocks)
            return n + mine.astype(jnp.int32)

        return lax.fori_loop(0, counts[b], of_slot, n)

    n = lax.fori_loop(0, blocks, of_block, jnp.int32(0))
    total[0] = n
    for extra in range(UNROLL):
        src[n + extra] = blocks
        tgt[n + extra] = own_blocks


def masked_rows(x, mask, b):
    piece = x[lax.shift_right_logical(b, 1)].reshape(BLOCK // 16, 16, HALF)
    lanes = mask[pl.ds(pl.multiple_of(lax.rem(b, 2) * 16, 16), 16), :]
    return (piece * lanes[None]).reshape(BLOCK, HALF)


def column_kernel(blocks, own_blocks, src, tgt, total, x, t, pot, gram, mask, out, peak, acc):
    peak[...] = jnp.full(peak.shape, NEG, F32)
    acc[...] = jnp.zeros(acc.shape, F32)
    pairs = total[0]

    def turn(step, carry):
        found = []
        for u in range(UNROLL):
            b_all = src[step * UNROLL + u]
            t_all = tgt[step * UNROLL + u]
            b = jnp.minimum(b_all, blocks - 1)
            tb = jnp.minimum(t_all, own_blocks - 1)
            rows = masked_rows(x, mask, b)
            pieces = []
            for h in range(2):
                line = pot[pl.ds(2 * b + h, 1), :] * SCALE
                pieces.append(jnp.transpose(jnp.broadcast_to(line, (HALF, HALF))))
            shift = jnp.concatenate(pieces, axis=0)
            for h in range(2):
                cols = t[pl.ds(pl.multiple_of(tb * BLOCK + h * HALF, HALF), HALF), :]
                s = nt(rows, cols) * SCALE + shift
                s = s.reshape(BLOCK // 8, 8, HALF)
                top = jnp.max(s, axis=0)
                part = jnp.sum(jnp.exp2(s - top[None]), axis=0)
                found.append((t_all, h, top, part))
        for t_all, h, top, part in found:
            at = (pl.ds(pl.multiple_of(t_all * 8, 8), 8), slice(h * HALF, (h + 1) * HALF))
            old = peak[at]
            new = jnp.maximum(old, top)
            acc[at] = acc[at] * jnp.exp2(old - new) + part * jnp.exp2(top - new)
            peak[at] = new
        return carry

    lax.fori_loop(0, (pairs + UNROLL - 1) // UNROLL, turn, 0)

    row = lax.broadcasted_iota(jnp.int32, (8, HALF), 0)
    moments = jnp.broadcast_to(gram[...], (8, HALF))

    def finish(p, carry):
        tile = jnp.where(row == 4, moments, 0.0)
        for r in range(4):
            at = (
                pl.ds(pl.multiple_of((2 * p + r // 2) * 8, 8), 8),
                slice((r % 2) * HALF, (r % 2 + 1) * HALF),
            )
            tops = peak[at]
            top = jnp.max(tops, axis=0, keepdims=True)
            whole = jnp.sum(acc[at] * jnp.exp2(tops - top), axis=0, keepdims=True)
            level = jnp.where(whole > 0.0, top + jnp.log2(jnp.maximum(whole, 1e-38)), NEG)
            tile = jnp.where(row == r, level, tile)
        out[p] = tile
        return carry

    lax.fori_loop(0, own_blocks // 2, finish, 0, unroll=4)


def combine_kernel(peers, arrived, out, gram):
    top = arrived[0]
    for p in range(1, peers):
        top = jnp.maximum(top, arrived[p])
    whole = jnp.zeros_like(top)
    plain = jnp.zeros_like(top)
    for p in range(peers):
        whole = whole + jnp.exp2(arrived[p] - top)
        plain = plain + arrived[p]
    level = (top + jnp.log2(whole))[:4]
    for p in range(peers):
        out[p] = level
    gram[...] = plain[4:5]


def row_kernel(blocks, own_blocks, src, tgt, total, x, t, pot, level, mask, out, acc):
    acc[...] = jnp.zeros(acc.shape, F32)
    pairs = total[0]

    def turn(step, carry):
        found = []
        for u in range(UNROLL):
            b_all = src[step * UNROLL + u]
            t_all = tgt[step * UNROLL + u]
            b = jnp.minimum(b_all, blocks - 1)
            tb = jnp.minimum(t_all, own_blocks - 1)
            rows = masked_rows(x, mask, b)
            lines = [pot[pl.ds(2 * b + h, 1), :] * SCALE for h in range(2)]
            line = jnp.concatenate(lines, axis=1)
            parts = None
            for h in range(2):
                cols = t[pl.ds(pl.multiple_of(tb * BLOCK + h * HALF, HALF), HALF), :]
                log_line = level[
                    lax.shift_right_logical(tb, 1), pl.ds(lax.rem(tb, 2) * 2 + h, 1), :
                ]
                shift = jnp.transpose(jnp.broadcast_to(log_line, (HALF, HALF)))
                s = nt(cols, rows) * SCALE + line
                e = jnp.exp2(s - jnp.concatenate([shift, shift], axis=1))
                part = jnp.sum(e.reshape(HALF // 8, 8, BLOCK), axis=0)
                parts = part if parts is None else parts + part
            found.append((b_all, parts))
        for b_all, parts in found:
            at = pl.ds(pl.multiple_of(b_all * 8, 8), 8)
            acc[at, :] = acc[at, :] + parts
        return carry

    lax.fori_loop(0, (pairs + UNROLL - 1) // UNROLL, turn, 0)

    def finish(p, carry):
        for half in range(2):
            at = pl.ds(pl.multiple_of((2 * p + half) * 8, 8), 8)
            sums = jnp.sum(acc[at, :], axis=0, keepdims=True)
            for h in range(2):
                out[p, 2 * half + h : 2 * half + h + 1, :] = sums[:, h * HALF : (h + 1) * HALF]
        return carry

    lax.fori_loop(0, blocks // 2, finish, 0, unroll=4)


def gradient_kernel(peers, ratio, arrived, steps, slopes, gradient, dots):
    mass = arrived[0]
    for p in range(1, peers):
        mass = mass + arrived[p]
    grad = 1.0 - ratio * mass
    gradient[...] = grad
    line = jnp.concatenate([grad[r : r + 1] for r in range(4)], axis=1)
    lane = lax.broadcasted_iota(jnp.int32, (8, HALF), 1)
    row = lax.broadcasted_iota(jnp.int32, (8, HALF), 0)
    step_dots = jnp.sum(steps[...] * line, axis=1, keepdims=True)
    slope_dots = jnp.sum(slopes[...] * line, axis=1, keepdims=True)
    spread = jnp.where(lane == row, step_dots, 0.0) + jnp.where(lane == row + 8, slope_dots, 0.0)
    value = jnp.sum(spread, axis=0, keepdims=True)
    for p in range(peers):
        dots[p] = value


def pass_on_kernel(peers, given, arrived, out):
    value = arrived[0]
    for p in range(1, peers):
        value = value + arrived[p]
    for p in range(given):
        out[p] = value


def recursion_kernel(stored, gram, out):
    lane = lax.broadcasted_iota(jnp.int32, (1, HALF), 1)

    def unit(k):
        return jnp.where(lane == k, 1.0, 0.0).astype(F32)

    def cross(k, m):
        return gram[0, 8 * k + m]

    def slope(k, m):
        return gram[0, 64 + 8 * k + m]

    def full(value):
        return jnp.full((1, HALF), value, F32)

    rho = [1.0 / full(cross(k, k)) for k in range(stored)]
    gamma = full(cross(stored - 1, stored - 1)) / full(slope(stored - 1, stored - 1))
    alpha = [None] * stored
    for k in reversed(range(stored)):
        value = unit(k)
        for m in range(k + 1, stored):
            value = value - cross(k, m) * alpha[m]
        alpha[k] = value * rho[k]
    delta = [None] * stored
    for k in range(stored):
        value = unit(8 + k)
        for m in range(stored):
            value = value - slope(k, m) * alpha[m]
        value = value * gamma
        for m in range(k):
            value = value + cross(m, k) * delta[m]
        delta[k] = alpha[k] - value * rho[k]
    for k in range(stored):
        out[k : k + 1, :] = -delta[k]
        out[8 + k : 9 + k, :] = gamma * alpha[k]
    out[16:17, :] = -gamma


def direction_kernel(peers, arrived, forms, gradient, steps, slopes, out):
    dots = arrived[0]
    for p in range(1, peers):
        dots = dots + arrived[p]
    weights = jnp.sum(forms[:16, :] * dots, axis=1, keepdims=True)
    mix = weights[:8] * steps[...] + weights[8:16] * slopes[...]
    mix = jnp.sum(mix, axis=0, keepdims=True)
    line = jnp.concatenate([mix[:, r * HALF : (r + 1) * HALF] for r in range(4)], axis=0)
    out[...] = forms[16:17, :] * gradient[...] + line


def per_device(sources, targets, potential, block_map, counts, step_history, slope_history):
    src_size, tgt_size = lax.axis_size(SRC), lax.axis_size(TGT)
    blocks = potential.shape[0] // BLOCK
    own_blocks = targets.shape[0] // BLOCK
    listed = block_map.shape[1]
    stored = step_history.shape[0]
    pieces = sources.shape[0] // BLOCK
    assert pieces == 2

    packed = jnp.concatenate([sources[:BLOCK], sources[BLOCK:]], axis=1)
    x = share(packed, TGT)
    t = jnp.concatenate([targets, targets], axis=1)
    pot = potential.reshape(-1, HALF)
    lane = jnp.arange(HALF, dtype=jnp.int32)[None, :] // 64
    mask_row = jnp.arange(32, dtype=jnp.int32)[:, None] // 16
    mask = (lane == mask_row).astype(jnp.bfloat16)

    highest = lax.Precision.HIGHEST
    cross = nt(step_history, slope_history, highest)
    slopes = nt(slope_history, slope_history, highest)
    moments = jnp.concatenate([cross.reshape(1, -1), slopes.reshape(1, -1)], axis=1)
    gram_part = jnp.sum(share(moments, TGT), axis=0)

    rank = lax.axis_index(TGT).astype(jnp.int32).reshape(1)
    slots = blocks * listed + UNROLL
    src, tgt, total = call(
        functools.partial(listing_kernel, blocks, own_blocks),
        (sds((slots,), jnp.int32), sds((slots,), jnp.int32), sds((1,), jnp.int32)),
        [SMEM] * 3,
        [SMEM] * 3,
    )(rank, block_map, counts)

    levels = call(
        functools.partial(column_kernel, blocks, own_blocks),
        sds((src_size, 8, HALF)),
        [SMEM] * 3 + [VMEM] * 5,
        VMEM,
        [pltpu.VMEM((8 * own_blocks + 8, BLOCK), F32)] * 2,
    )(src, tgt, total, x, t, pot, gram_part, mask)

    level, gram = call(
        functools.partial(combine_kernel, src_size),
        (sds((src_size, 4, HALF)), sds((1, HALF))),
        [VMEM],
        [VMEM] * 2,
    )(swap(levels, SRC))
    level = swap(level, SRC)
    target_potential = (-entropy * LN2) * level.reshape(-1)

    forms = call(
        functools.partial(recursion_kernel, stored), sds((24, HALF)), [SMEM], VMEM
    )(gram)

    masses = call(
        functools.partial(row_kernel, blocks, own_blocks),
        sds((tgt_size, 4, HALF)),
        [SMEM] * 3 + [VMEM] * 5,
        VMEM,
        [pltpu.VMEM((8 * blocks + 8, BLOCK), F32)],
    )(src, tgt, total, x, t, pot, level, mask)

    ratio = blocks * src_size / (own_blocks * tgt_size)
    gradient, dots = call(
        functools.partial(gradient_kernel, tgt_size, ratio),
        (sds((4, HALF)), sds((tgt_size, 1, HALF))),
        [VMEM] * 3,
        [VMEM] * 2,
    )(swap(masses, TGT), step_history, slope_history)
    dots = call(
        functools.partial(pass_on_kernel, tgt_size, src_size),
        sds((src_size, 1, HALF)),
        [VMEM],
        VMEM,
    )(swap(dots, TGT))
    direction = call(
        functools.partial(direction_kernel, src_size), sds((4, HALF)), [VMEM] * 5, VMEM
    )(swap(dots, SRC), forms, gradient, step_history, slope_history)
    return (gradient.reshape(-1), direction.reshape(-1), target_potential)


def solution(mesh):
    split = Mesh(mesh.devices.reshape(4, 8, 8, 2), ("src_0", "src_1", "tgt_0", "tgt_1"))
    in_specs = (
        P(SRC_TGT, None),
        P(TGT, None),
        P(SRC),
        P(SRC, None),
        P(SRC),
        P(None, SRC_TGT),
        P(None, SRC_TGT),
    )
    out_specs = (P(SRC_TGT), P(SRC_TGT), P(TGT))
    return jax.shard_map(
        per_device, mesh=split, in_specs=in_specs, out_specs=out_specs, check_vma=False
    )
```

profile of v0, /device:TPU:1, one launch (start us, length us, event | category | flops | bytes accessed | tf_op | source)
XLA Modules:
  0.0 149.1 jit_solution(17056933645426317248)
XLA Ops:
  0.6 0.0 copy-start.6
  0.6 1.0 fusion.2
  1.7 0.9 fusion.1
  2.5 0.1 reshape.108
  2.6 0.1 reshape.109
  2.7 0.1 maximum_bitcast_fusion
  2.8 0.6 broadcast_in_dim.8
  3.4 10.1 %all-to-all-start.1 = ((f32[16,1,128]{2,1,0:T(1,128)}), f32[16,1,128]{2,1,0:T(1,128)S(1)}, u32[]{:S(2)}, u32[]{:S(2)}) async-start(f32[16,1,128]{2,1,0:T(1,128)} %broadcast_in_dim.8), calls=%async_computation.1 | async-start | bytes 16384 | tf_op jit(solution)/shard_map/all_to_all | solution.py:51
  13.6 0.8 fusion
  14.4 0.1 copy.19
  14.5 6.1 %all-to-all-done.1 = f32[16,1,128]{2,1,0:T(1,128)S(1)} async-done(((f32[16,1,128]{2,1,0:T(1,128)}), f32[16,1,128]{2,1,0:T(1,128)S(1)}, u32[]{:S(2)}, u32[]{:S(2)}) %all-to-all-start.1) | async-done | bytes 8224 | tf_op jit(solution)/shard_map/all_to_all | solution.py:51
  20.5 1.3 broadcast_in_dim.6
  21.8 0.0 copy-start.5
  21.8 4.2 %all-to-all-start = ((bf16[16,256,128]{2,1,0:T(8,128)(2,1)}), bf16[16,256,128]{2,1,0:T(8,128)(2,1)S(1)}, u32[]{:S(2)}, u32[]{:S(2)}) async-start(bf16[16,256,128]{2,1,0:T(8,128)(2,1)} %broadcast_in_dim.6), calls=%async_computation | async-start | bytes 2097152 | tf_op jit(solution)/shard_map/all_to_all | solution.py:51
  26.0 0.1 compare_convert_fusion.mask
  26.1 0.8 copy.18.block_map
  26.9 0.0 copy-done.6
  26.9 3.2 %copy.20 = bf16[16384,64]{1,0:T(8,128)(2,1)} copy(bf16[16384,64]{0,1:T(8,128)(2,1)S(1)} %copy-done.6) | data formatting | bytes 4194304 | tf_op args[1]
  30.1 0.0 copy-done.5
  30.1 7.1 %shard_map.94 = (s32[642]{0:T(1024)S(1)}, s32[642]{0:T(1024)S(1)}, s32[1]{0:T(128)}) custom-call(s32[1]{0:T(128)} %bitcast.rank, s32[32,20]{1,0:T(8,128)S(1)} %copy.18.block_map, s32[32]{0:T(128)S(1)} %copy-done.5), custom_call_target="tpu_custom_call" | custom-call | tf_op jit(solution)/shard_map/pallas_call | solution.py:298
  37.2 0.0 copy-start.3
  37.2 6.8 %pad_maximum_fusion.t = bf16[16384,128]{1,0:T(8,128)(2,1)} fusion(bf16[16384,64]{1,0:T(8,128)(2,1)} %copy.20), kind=kLoop, calls=%fused_computation | loop fusion | flops 8388608 | bytes 6291456 | tf_op jit(solution)/shard_map/concatenate | solution.py:284
  44.1 9.9 %all-to-all-done.x = bf16[16,256,128]{2,1,0:T(8,128)(2,1)S(1)} async-done(((bf16[16,256,128]{2,1,0:T(8,128)(2,1)}), bf16[16,256,128]{2,1,0:T(8,128)(2,1)S(1)}, u32[]{:S(2)}, u32[]{:S(2)}) %all-to-all-start) | async-done | bytes 1048608 | tf_op jit(solution)/shard_map/all_to_all | solution.py:51
  54.0 0.0 copy-done.3
  54.0 0.0 copy-start
  54.0 2.2 %copy-done = bf16[16384,128]{1,0:T(8,128)(2,1)S(1)} copy-done((bf16[16384,128]{1,0:T(8,128)(2,1)S(1)}, bf16[16384,128]{1,0:T(8,128)(2,1)}, u32[]{:S(2)}) %copy-start) | copy-done | bytes 4194328
  56.2 7.1 %shard_map.95 = f32[32,8,128]{2,1,0:T(8,128)S(1)} custom-call(s32[642]{0:T(1024)S(1)} %get-tuple-element.10.src, s32[642]{0:T(1024)S(1)} %get-tuple-element.11.tgt, s32[1]{0:T(128)} %get-tuple-element.12.total, bf16[16,256,128]{2,1,0:T(8,128)(2,1)S(1)} %all-to-all-done.x, bf16[16384,128]{1,0:T(8,128)(2,1)S(1)} %copy-done, f32[64,128]{1,0:T(8,128)S(1)} %bitcast.13, ...), custom_call_target="tpu_custom_call" | custom-call | tf_op jit(solution)/shard_map/pallas_call | solution.py:305
  63.3 0.0 copy-start.1
  63.3 0.0 copy-start.2
  63.3 19.7 %all_to_all.35.arrived = f32[32,8,128]{2,1,0:T(8,128)S(1)} all-to-all(f32[32,8,128]{2,1,0:T(8,128)S(1)} %shard_map.95), channel_id=1, replica_groups=mesh['src_0'=4,'src_1'=8,'tgt_0'=8,'tgt_1'=2] {'src_0','src_1'}, dimensions={0} | all-to-all | bytes 262144 | tf_op jit(solution)/shard_map/all_to_all | solution.py:51
  83.0 0.1 shard_map.96
  83.1 13.3 %all_to_all.36.level = f32[32,4,128]{2,1,0:T(4,128)S(1)} all-to-all(f32[32,4,128]{2,1,0:T(4,128)S(1)} %get-tuple-element.13), channel_id=1, replica_groups=mesh['src_0'=4,'src_1'=8,'tgt_0'=8,'tgt_1'=2] {'src_0','src_1'}, dimensions={0} | all-to-all | bytes 131072 | tf_op jit(solution)/shard_map/all_to_all | solution.py:51
  96.4 5.7 %shard_map.97 = f32[16,4,128]{2,1,0:T(4,128)S(1)} custom-call(s32[642]{0:T(1024)S(1)} %get-tuple-element.10.src, s32[642]{0:T(1024)S(1)} %get-tuple-element.11.tgt, s32[1]{0:T(128)} %get-tuple-element.12.total, bf16[16,256,128]{2,1,0:T(8,128)(2,1)S(1)} %all-to-all-done.x, bf16[16384,128]{1,0:T(8,128)(2,1)S(1)} %copy-done, f32[64,128]{1,0:T(8,128)S(1)} %bitcast.14, ...), custom_call_target="tpu_custom_call" | custom-call | tf_op jit(solution)/shard_map/pallas_call | solution.py:326
  102.1 17.4 %all_to_all.37.arrived = f32[16,4,128]{2,1,0:T(4,128)S(1)} all-to-all(f32[16,4,128]{2,1,0:T(4,128)S(1)} %shard_map.97), channel_id=1, replica_groups=mesh['src_0'=4,'src_1'=8,'tgt_0'=8,'tgt_1'=2] {'tgt_0','tgt_1'}, dimensions={0} | all-to-all | bytes 65536 | tf_op jit(solution)/shard_map/all_to_all | solution.py:51
  119.5 0.0 copy-done.1
  119.5 0.0 copy-done.2
  119.5 0.7 shard_map.98
  120.2 3.7 %all-to-all-start.5 = ((f32[16,1,128]{2,1,0:T(1,128)}), f32[16,1,128]{2,1,0:T(1,128)S(1)}, u32[]{:S(2)}, u32[]{:S(2)}) async-start(f32[16,1,128]{2,1,0:T(1,128)} %get-tuple-element.15), calls=%async_computation.5 | async-start | bytes 16384 | tf_op jit(solution)/shard_map/all_to_all | solution.py:51
  123.9 0.6 shard_map.100.forms
  124.5 6.3 %all-to-all-done.5.arrived = f32[16,1,128]{2,1,0:T(1,128)S(1)} async-done(((f32[16,1,128]{2,1,0:T(1,128)}), f32[16,1,128]{2,1,0:T(1,128)S(1)}, u32[]{:S(2)}, u32[]{:S(2)}) %all-to-all-start.5) | async-done | bytes 8224 | tf_op jit(solution)/shard_map/all_to_all | solution.py:51
  130.8 0.6 shard_map.99
  131.5 7.6 %all-to-all-start.6 = ((f32[32,1,128]{2,1,0:T(1,128)}), f32[32,1,128]{2,1,0:T(1,128)S(1)}, u32[]{:S(2)}, u32[]{:S(2)}) async-start(f32[32,1,128]{2,1,0:T(1,128)} %shard_map.99), calls=%async_computation.6 | async-start | bytes 32768 | tf_op jit(solution)/shard_map/all_to_all | solution.py:51
  139.1 0.6 broadcast_multiply_fusion
  139.8 8.0 %all-to-all-done.6.arrived = f32[32,1,128]{2,1,0:T(1,128)S(1)} async-done(((f32[32,1,128]{2,1,0:T(1,128)}), f32[32,1,128]{2,1,0:T(1,128)S(1)}, u32[]{:S(2)}, u32[]{:S(2)}) %all-to-all-start.6) | async-done | bytes 16416 | tf_op jit(solution)/shard_map/all_to_all | solution.py:51
  147.7 0.0 copy-start.4
  147.7 0.7 copy-done.4
  148.4 0.7 shard_map.101
  (4 shorter events, 0.0 us)
Async XLA Ops:
  0.6 26.3 %copy-start.6 = (bf16[16384,64]{0,1:T(8,128)(2,1)S(1)}, bf16[16384,64]{0,1:T(8,128)(2,1)}, u32[]{:S(2)}) copy-start(bf16[16384,64]{0,1:T(8,128)(2,1)} %param.8) | copy-start | bytes 6291460
  3.4 17.1 %all-to-all-start.1 = ((f32[16,1,128]{2,1,0:T(1,128)}), f32[16,1,128]{2,1,0:T(1,128)S(1)}, u32[]{:S(2)}, u32[]{:S(2)}) async-start(f32[16,1,128]{2,1,0:T(1,128)} %broadcast_in_dim.8), calls=%async_computation.1 | async-start | bytes 16384 | tf_op jit(solution)/shard_map/all_to_all | solution.py:51
  21.8 8.3 %copy-start.5 = (s32[32]{0:T(128)S(1)}, s32[32]{0:T(128)}, u32[]{:S(2)}) copy-start(s32[32]{0:T(128)} %counts.1) | copy-start | bytes 388
  21.8 32.2 %all-to-all-start = ((bf16[16,256,128]{2,1,0:T(8,128)(2,1)}), bf16[16,256,128]{2,1,0:T(8,128)(2,1)S(1)}, u32[]{:S(2)}, u32[]{:S(2)}) async-start(bf16[16,256,128]{2,1,0:T(8,128)(2,1)} %broadcast_in_dim.6), calls=%async_computation | async-start | bytes 2097152 | tf_op jit(solution)/shard_map/all_to_all | solution.py:51
  37.2 16.8 %copy-start.3 = (f32[8192]{0:T(1024)S(1)}, f32[8192]{0:T(1024)}, u32[]{:S(2)}) copy-start(f32[8192]{0:T(1024)} %param.9) | copy-start | bytes 98308
  54.0 2.2 %copy-start = (bf16[16384,128]{1,0:T(8,128)(2,1)S(1)}, bf16[16384,128]{1,0:T(8,128)(2,1)}, u32[]{:S(2)}) copy-start(bf16[16384,128]{1,0:T(8,128)(2,1)} %pad_maximum_fusion.t) | copy-start | bytes 12582916
  63.3 56.2 %copy-start.1 = (f32[8,512]{1,0:T(8,128)S(1)}, f32[8,512]{1,0:T(8,128)}, u32[]{:S(2)}) copy-start(f32[8,512]{1,0:T(8,128)} %slopes.3) | copy-start | bytes 49156
  63.3 56.2 %copy-start.2 = (f32[8,512]{1,0:T(8,128)S(1)}, f32[8,512]{1,0:T(8,128)}, u32[]{:S(2)}) copy-start(f32[8,512]{1,0:T(8,128)} %steps.3) | copy-start | bytes 49156
  120.2 10.6 %all-to-all-start.5 = ((f32[16,1,128]{2,1,0:T(1,128)}), f32[16,1,128]{2,1,0:T(1,128)S(1)}, u32[]{:S(2)}, u32[]{:S(2)}) async-start(f32[16,1,128]{2,1,0:T(1,128)} %get-tuple-element.15), calls=%async_computation.5 | async-start | bytes 16384 | tf_op jit(solution)/shard_map/all_to_all | solution.py:51
  131.5 16.3 %all-to-all-start.6 = ((f32[32,1,128]{2,1,0:T(1,128)}), f32[32,1,128]{2,1,0:T(1,128)S(1)}, u32[]{:S(2)}, u32[]{:S(2)}) async-start(f32[32,1,128]{2,1,0:T(1,128)} %shard_map.99), calls=%async_computation.6 | async-start | bytes 32768 | tf_op jit(solution)/shard_map/all_to_all | solution.py:51
  147.7 0.7 copy-start.4
where the time goes:
time: 150 us; the launch traced here: 149 us
  blocking collectives  50.4 us (34%)
  waiting for transfers between devices  30.3 us (20%)
  starting transfers between devices  25.7 us (17%)
  Pallas kernels  22.6 us (15%)
  local copies, waits for them, and re-layouts  9.84 us (7%)
  other arithmetic  7.66 us (5%)
  matrix products  1.9 us (1%)
    all_to_all x3, blocking collectives, swap(): return lax.all_to_all(x, axis, 0, 0, tiled=True)  50.4 us
    all_to_all x4, waiting for transfers between devices, swap(): return lax.all_to_all(x, axis, 0, 0, tiled=True)  30.3 us
    all_to_all x4, starting transfers between devices, swap(): return lax.all_to_all(x, axis, 0, 0, tiled=True)  25.7 us
    pallas_call x1, Pallas kernels, per_device(): call(functools.partial(listing_kernel, blocks, own_blocks), (sds((slots,)...  7.08 us
    pallas_call x1, Pallas kernels, per_device(): call(functools.partial(column_kernel, blocks, own_blocks), sds((src_size,...  7.05 us
    unnamed x16, local copies, waits for them, and re-layouts  6.89 us
    concatenate x1, other arithmetic, per_device(): t = jnp.concatenate([targets, targets], axis=1)  6.83 us
    pallas_call x1, Pallas kernels, per_device(): call(functools.partial(row_kernel, blocks, own_blocks), sds((tgt_size, 4,...  5.71 us
  transfers between devices with their start and end apart: 4, of which 4 were waited for; matrix products, arithmetic and copies ran while one was open for 8% of the time, Pallas kernels for 5%

commit v1 on v0

v1 whole, which is shorter than its diff:
```python
import functools

import jax
import jax.numpy as jnp
from jax import lax
from jax.experimental import pallas as pl
from jax.experimental.pallas import tpu as pltpu
from jax.sharding import Mesh
from jax.sharding import PartitionSpec as P

BLOCK = 256
HALF = 128
TGT = ("tgt_0", "tgt_1")
SRC = ("src_0", "src_1")
SRC_TGT = ("src_0", "src_1", "tgt_0", "tgt_1")
NEG = -1e30
LOG2E = 1.4426950408889634
LN2 = 0.6931471805599453
entropy = 0.5
SCALE = LOG2E / entropy
UNROLL = 2
F32 = jnp.float32

VMEM = pl.BlockSpec(memory_space=pltpu.VMEM)
SMEM = pl.BlockSpec(memory_space=pltpu.SMEM)


def call(body, out_shape, ins, outs, scratch=(), cost=None):
    return pl.pallas_call(
        body,
        out_shape=out_shape,
        in_specs=ins,
        out_specs=outs,
        scratch_shapes=list(scratch),
        cost_estimate=cost,
        compiler_params=pltpu.CompilerParams(vmem_limit_bytes=24 * 2**20),
    )


def sds(shape, dtype=F32):
    return jax.ShapeDtypeStruct(shape, dtype)


def nn(a, b):
    return jnp.dot(a, b, preferred_element_type=F32)


def nt(a, b, precision=None):
    return lax.dot_general(
        a, b, (((1,), (1,)), ((), ())), precision=precision, preferred_element_type=F32
    )


def swap(x, axis):
    return lax.all_to_all(x, axis, 0, 0, tiled=True)


def share(x, axis):
    return swap(jnp.broadcast_to(x[None], (lax.axis_size(axis), *x.shape)), axis)


def listing_kernel(blocks, own_blocks, rank, block_map, counts, src, tgt, total):
    first = rank[0] * own_blocks

    def of_block(b, n):
        count = counts[b]
        for k in range(block_map.shape[1]):
            local = block_map[b, k] - first
            src[n] = b
            tgt[n] = local
            mine = (k < count) & (local >= 0) & (local < own_blocks)
            n = n + mine.astype(jnp.int32)
        return n

    n = lax.fori_loop(0, blocks, of_block, jnp.int32(0))
    total[0] = n
    for extra in range(UNROLL):
        src[n + extra] = blocks
        tgt[n + extra] = own_blocks


def lay_out(rank, mine, other, mask, rows):
    core = rank[1]
    for arrived, side in ((mine, core), (other, 1 - core)):
        for y in range(arrived.shape[0]):
            piece = arrived[y].reshape(BLOCK // 16, 16, HALF)
            for half in range(2):
                lanes = mask[half * 16 : half * 16 + 16, :]
                rows[4 * y + 2 * side + half] = (piece * lanes[None]).reshape(BLOCK, HALF)


def column_kernel(
    blocks, own_blocks, rank, src, tgt, total, mine, other, t, pot, mask, out, x, peak, acc
):
    lay_out(rank, mine, other, mask, x)
    peak[...] = jnp.full(peak.shape, NEG, F32)
    acc[...] = jnp.zeros(acc.shape, F32)
    live = total[0]

    def turn(step, carry):
        found = []
        for u in range(UNROLL):
            b_all = src[step * UNROLL + u]
            t_all = tgt[step * UNROLL + u]
            b = jnp.minimum(b_all, blocks - 1)
            tb = jnp.minimum(t_all, own_blocks - 1)
            rows = x[b]
            pieces = []
            for h in range(2):
                line = pot[pl.ds(2 * b + h, 1), :] * SCALE
                pieces.append(jnp.transpose(jnp.broadcast_to(line, (HALF, HALF))))
            shift = jnp.concatenate(pieces, axis=0)
            for h in range(2):
                cols = t[:, pl.ds(pl.multiple_of(tb * BLOCK + h * HALF, HALF), HALF)]
                s = nn(rows, cols) * SCALE + shift
                s = s.reshape(BLOCK // 8, 8, HALF)
                top = jnp.max(s, axis=0)
                part = jnp.sum(jnp.exp2(s - top[None]), axis=0)
                found.append((t_all, h, top, part))
        for t_all, h, top, part in found:
            at = (pl.ds(pl.multiple_of(t_all * 8, 8), 8), slice(h * HALF, (h + 1) * HALF))
            old = peak[at]
            new = jnp.maximum(old, top)
            acc[at] = acc[at] * jnp.exp2(old - new) + part * jnp.exp2(top - new)
            peak[at] = new
        return carry

    lax.fori_loop(0, (live + UNROLL - 1) // UNROLL, turn, 0)

    def finish(p, carry):
        for r in range(4):
            at = (
                pl.ds(pl.multiple_of((2 * p + r // 2) * 8, 8), 8),
                slice((r % 2) * HALF, (r % 2 + 1) * HALF),
            )
            tops = peak[at]
            top = jnp.max(tops, axis=0, keepdims=True)
            whole = jnp.sum(acc[at] * jnp.exp2(tops - top), axis=0, keepdims=True)
            level = jnp.where(whole > 0.0, top + jnp.log2(jnp.maximum(whole, 1e-38)), NEG)
            out[p, r : r + 1, :] = level
        return carry

    lax.fori_loop(0, own_blocks // 2, finish, 0, unroll=4)


def combine_kernel(peers, arrived, out):
    top = arrived[0]
    for p in range(1, peers):
        top = jnp.maximum(top, arrived[p])
    whole = jnp.zeros_like(top)
    for p in range(peers):
        whole = whole + jnp.exp2(arrived[p] - top)
    level = top + jnp.log2(whole)
    for p in range(peers):
        out[p] = level


def turn_kernel(t, out):
    def turn(c, carry):
        at = pl.ds(pl.multiple_of(c * HALF, HALF), HALF)
        out[at, :] = jnp.transpose(t[:, at])
        return carry

    lax.fori_loop(0, t.shape[1] // HALF, turn, 0, unroll=4)


def moments_kernel(peers, stored, pairs, out, square):
    total = jnp.zeros((2 * stored, 2 * stored), F32)
    for p in range(peers):
        rows = pairs[p, : 2 * stored, :]
        total = total + nt(rows, rows, lax.Precision.HIGHEST)
    square[...] = jnp.zeros(square.shape, F32)
    square[:, : 2 * stored] = total
    lane = lax.broadcasted_iota(jnp.int32, (1, HALF), 1)
    line = jnp.zeros((1, HALF), F32)
    for k in range(stored):
        for row, place in ((k, cross_lane(k, k)), (stored + k, slope_lane(k, k))):
            kept = (lane >= stored + k) & (lane < 2 * stored)
            part = jnp.where(kept, square[row : row + 1, :], 0.0)
            line = line + pltpu.roll(part, (place - stored - k) % HALF, 1)
    out[...] = line


def row_kernel(
    blocks, own_blocks, ratio, peers, src, tgt, total, x, t, pot, level, pairs, out, acc
):
    acc[...] = jnp.zeros(acc.shape, F32)
    live = total[0]

    def turn(step, carry):
        found = []
        for u in range(UNROLL):
            b_all = src[step * UNROLL + u]
            t_all = tgt[step * UNROLL + u]
            b = jnp.minimum(b_all, blocks - 1)
            tb = jnp.minimum(t_all, own_blocks - 1)
            rows = x[b]
            lines = [pot[pl.ds(2 * b + h, 1), :] * SCALE for h in range(2)]
            line = jnp.concatenate(lines, axis=1)
            parts = None
            for h in range(2):
                cols = t[pl.ds(pl.multiple_of(tb * BLOCK + h * HALF, HALF), HALF), :]
                log_line = level[
                    lax.shift_right_logical(tb, 1), pl.ds(lax.rem(tb, 2) * 2 + h, 1), :
                ]
                shift = jnp.transpose(jnp.broadcast_to(log_line, (HALF, HALF)))
                s = nt(cols, rows) * SCALE + line
                e = jnp.exp2(s - jnp.concatenate([shift, shift], axis=1))
                part = jnp.sum(e.reshape(HALF // 8, 8, BLOCK), axis=0)
                parts = part if parts is None else parts + part
            found.append((b_all, parts))
        for b_all, parts in found:
            at = pl.ds(pl.multiple_of(b_all * 8, 8), 8)
            acc[at, :] = acc[at, :] + parts
        return carry

    lax.fori_loop(0, (live + UNROLL - 1) // UNROLL, turn, 0)

    rows_kept = pairs.shape[1] // 2
    lane = lax.broadcasted_iota(jnp.int32, (rows_kept, HALF), 1)
    row = lax.broadcasted_iota(jnp.int32, (rows_kept, HALF), 0)
    dots = jnp.zeros((rows_kept, HALF), F32)
    for p in range(blocks // 2):
        for half in range(2):
            at = pl.ds((2 * p + half) * 8, 8)
            part = 1.0 / peers - ratio * jnp.sum(acc[at, :], axis=0, keepdims=True)
            for h in range(2):
                q = 2 * half + h
                line = part[:, h * HALF : (h + 1) * HALF]
                out[p, q : q + 1, :] = line
                dots = dots + pairs[p, :rows_kept, q * HALF : (q + 1) * HALF] * line
    spread = jnp.where(lane == row, jnp.sum(dots, axis=1, keepdims=True), 0.0)
    value = jnp.sum(spread, axis=0, keepdims=True)
    for p in range(blocks // 2):
        out[p, 4:5, :] = value


def gradient_kernel(peers, src_size, arrived, moments, gradient, dots):
    whole = arrived[0]
    for p in range(1, peers):
        whole = whole + arrived[p]
    gradient[...] = whole[:4]
    value = whole[4:5] + moments[...]
    for p in range(src_size):
        dots[p] = value


def cross_lane(k, m):
    return 16 + 8 * k - k * (k - 1) // 2 + m - k


def slope_lane(k, m):
    k, m = min(k, m), max(k, m)
    return 52 + 8 * k - k * (k - 1) // 2 + m - k


def direction_kernel(peers, stored, arrived, gradient, steps, slopes, out):
    sums = arrived[0]
    for p in range(1, peers):
        sums = sums + arrived[p]

    def lane(c):
        return jnp.broadcast_to(sums[:, c : c + 1], (1, HALF))

    cross = [[lane(cross_lane(k, m)) if m >= k else None for m in range(stored)] for k in range(stored)]
    slope = [[lane(slope_lane(k, m)) for m in range(stored)] for k in range(stored)]
    rho = [1.0 / cross[k][k] for k in range(stored)]
    gamma = cross[stored - 1][stored - 1] / slope[stored - 1][stored - 1]
    left = [lane(k) for k in range(stored)]
    alpha = [None] * stored
    for k in reversed(range(stored)):
        alpha[k] = left[k] * rho[k]
        for j in range(k):
            left[j] = left[j] - alpha[k] * cross[j][k]
    left = [lane(stored + k) for k in range(stored)]
    for k in reversed(range(stored)):
        left = [left[j] - alpha[k] * slope[j][k] for j in range(stored)]
    left = [gamma * value for value in left]
    delta = [None] * stored
    for k in range(stored):
        delta[k] = alpha[k] - left[k] * rho[k]
        for j in range(k + 1, stored):
            left[j] = left[j] + delta[k] * cross[k][j]
    of_steps = jnp.concatenate([-delta[k] for k in range(stored)], axis=0)
    of_slopes = jnp.concatenate([gamma * alpha[k] for k in range(stored)], axis=0)
    for r in range(4):
        at = slice(r * HALF, (r + 1) * HALF)
        mix = jnp.sum(of_steps * steps[:, at] + of_slopes * slopes[:, at], axis=0, keepdims=True)
        out[r : r + 1, :] = mix - gamma * gradient[r : r + 1, :]


def per_device(sources, targets, potential, block_map, counts, step_history, slope_history):
    src_size, tgt_size = lax.axis_size(SRC), lax.axis_size(TGT)
    blocks = potential.shape[0] // BLOCK
    own_blocks = targets.shape[0] // BLOCK
    listed = block_map.shape[1]
    stored = step_history.shape[0]
    pieces = sources.shape[0] // BLOCK
    assert pieces == 2

    packed = jnp.concatenate([sources[:BLOCK], sources[BLOCK:]], axis=1)
    mine = share(packed, TGT[0])
    core = lax.axis_index(TGT[1])
    ttt = targets.T
    t = jnp.concatenate([ttt, ttt], axis=0)
    pot = potential.reshape(-1, HALF)
    lane = jnp.arange(HALF, dtype=jnp.int32)[None, :] // 64
    mask_row = jnp.arange(32, dtype=jnp.int32)[:, None] // 16
    mask = (lane == mask_row).astype(jnp.bfloat16)

    rank = jnp.stack([lax.axis_index(TGT), core]).astype(jnp.int32)
    slots = blocks * listed + UNROLL
    src, tgt, total = call(
        functools.partial(listing_kernel, blocks, own_blocks),
        (sds((slots,), jnp.int32), sds((slots,), jnp.int32), sds((1,), jnp.int32)),
        [SMEM] * 3,
        [SMEM] * 3,
    )(rank, block_map, counts)

    turned = call(turn_kernel, sds((targets.shape[0], HALF), jnp.bfloat16), [VMEM], VMEM)(t)
    other = lax.ppermute(mine, TGT[1], [(0, 1), (1, 0)])
    mine, other, t, turned = lax.optimization_barrier((mine, other, t, turned))
    history = jnp.concatenate([step_history, slope_history] * 2, axis=0)
    pairs = lax.all_gather(history, TGT)

    levels, x = call(
        functools.partial(column_kernel, blocks, own_blocks),
        (sds((src_size, 4, HALF)), sds((blocks, BLOCK, HALF), jnp.bfloat16)),
        [SMEM] * 4 + [VMEM] * 5,
        [VMEM] * 2,
        [pltpu.VMEM((8 * own_blocks + 8, BLOCK), F32)] * 2,
        pl.CostEstimate(flops=10**10, bytes_accessed=2 * 10**7, transcendentals=4 * 10**6),
    )(rank, src, tgt, total, mine, other, t, pot, mask)

    arrived = swap(levels, SRC)

    level = call(
        functools.partial(combine_kernel, src_size),
        sds((src_size, 4, HALF)),
        [VMEM],
        VMEM,
    )(arrived)
    level = swap(level, SRC)
    target_potential = (-entropy * LN2) * level.reshape(-1)

    moments = call(
        functools.partial(moments_kernel, tgt_size, stored),
        sds((1, HALF)),
        [VMEM],
        VMEM,
        [pltpu.VMEM((2 * stored, HALF), F32)],
    )(pairs)

    ratio = blocks * src_size / (own_blocks * tgt_size)
    parts = call(
        functools.partial(row_kernel, blocks, own_blocks, ratio, tgt_size),
        sds((tgt_size, 8, HALF)),
        [SMEM] * 3 + [VMEM] * 5,
        VMEM,
        [pltpu.VMEM((8 * blocks + 8, BLOCK), F32)],
        pl.CostEstimate(flops=10**10, bytes_accessed=2 * 10**7, transcendentals=4 * 10**6),
    )(src, tgt, total, x, turned, pot, level, pairs)

    gradient, dots = call(
        functools.partial(gradient_kernel, tgt_size, src_size),
        (sds((4, HALF)), sds((src_size, 1, HALF))),
        [VMEM] * 2,
        [VMEM] * 2,
    )(swap(parts, TGT), moments)
    direction = call(
        functools.partial(direction_kernel, src_size, stored), sds((4, HALF)), [VMEM] * 4, VMEM
    )(swap(dots, SRC), gradient, step_history, slope_history)
    return (gradient.reshape(-1), direction.reshape(-1), target_potential)


def solution(mesh):
    split = Mesh(mesh.devices.reshape(4, 8, 8, 2), ("src_0", "src_1", "tgt_0", "tgt_1"))
    in_specs = (
        P(SRC_TGT, None),
        P(TGT, None),
        P(SRC),
        P(SRC, None),
        P(SRC),
        P(None, SRC_TGT),
        P(None, SRC_TGT),
    )
    out_specs = (P(SRC_TGT), P(SRC_TGT), P(TGT))
    return jax.shard_map(
        per_device, mesh=split, in_specs=in_specs, out_specs=out_specs, check_vma=False
    )
```

time: 150 us -> 137 us (0.913)
  blocking collectives: 50.4 us -> 33.6 us
  waiting for transfers between devices: 30.3 us -> 16.3 us
  between operations: 0.73 us -> 14.1 us
  starting transfers between devices: 25.7 us -> 28.8 us
  local copies, waits for them, and re-layouts: 9.84 us -> 12.3 us
  Pallas kernels: 22.6 us -> 24.6 us
  matrix products: 1.9 us -> 0 us
    all_to_all x3 -> x2, blocking collectives: 50.4 us -> 33.6 us  [swap(): return lax.all_to_all(x, axis, 0, 0, tiled=True)]
    all_to_all x4 -> x3, waiting for transfers between devices: 30.3 us -> 16.3 us  [swap(): return lax.all_to_all(x, axis, 0, 0, tiled=True)]
    ppermute x0 -> x1, starting transfers between devices: none -> 5.59 us  [per_device(): other = lax.ppermute(mine, TGT[1], [(0, 1), (1, 0)])]
    pallas_call x7, Pallas kernels: 15.5 us -> 20.2 us  [the longest x1 7.75 us: per_device(): call(functools.partial(column_kernel, blocks, own_blocks), (sds((src_size...]
    unnamed x16 -> x25, local copies, waits for them, and re-layouts: 6.89 us -> 10.6 us
    pallas_call x1, Pallas kernels: 7.08 us -> 4.37 us  [per_device(): call(functools.partial(listing_kernel, blocks, own_blocks), (sds((slots,)...]
    all_to_all x4 -> x3, starting transfers between devices: 25.7 us -> 23.2 us  [swap(): return lax.all_to_all(x, axis, 0, 0, tiled=True)]
    dot_general x2 -> x0, matrix products: 1.9 us -> none  [nt(): lax.dot_general(a, b, (((1,), (1,)), ((), ())), precision=precision, pref...]
  transfers between devices with their start and end apart: 4 -> 5, of which waited for: 4 -> 3; matrix products, arithmetic and copies ran while one was open for 8% -> 5% of each run, Pallas kernels for 5% -> 12%
where the time goes in v1:
time: 137 us
  blocking collectives  33.6 us (25%)
  starting transfers between devices  28.8 us (21%)
  Pallas kernels  24.6 us (18%)
  waiting for transfers between devices  16.3 us (12%)
  between operations  14.1 us (10%)
  local copies, waits for them, and re-layouts  12.3 us (9%)
  other arithmetic  6.78 us (5%)
    all_to_all x2, blocking collectives, swap(): return lax.all_to_all(x, axis, 0, 0, tiled=True)  33.6 us
    all_to_all x3, starting transfers between devices, swap(): return lax.all_to_all(x, axis, 0, 0, tiled=True)  23.2 us
    all_to_all x3, waiting for transfers between devices, swap(): return lax.all_to_all(x, axis, 0, 0, tiled=True)  16.3 us
    unnamed x25, local copies, waits for them, and re-layouts  10.6 us
    pallas_call x1, Pallas kernels, per_device(): call(functools.partial(column_kernel, blocks, own_blocks), (sds((src_size...  7.75 us
    pallas_call x1, Pallas kernels, per_device(): call(functools.partial(row_kernel, blocks, own_blocks, ratio, tgt_size),...  7.01 us
    ppermute x1, starting transfers between devices, per_device(): other = lax.ppermute(mine, TGT[1], [(0, 1), (1, 0)])  5.59 us
    concatenate x1, other arithmetic, per_device(): t = jnp.concatenate([ttt, ttt], axis=0)  4.54 us
  transfers between devices with their start and end apart: 5, of which 3 were waited for; matrix products, arithmetic and copies ran while one was open for 5% of the time, Pallas kernels for 12%

profile of v1, /device:TPU:1, one launch (start us, length us, event | category | flops | bytes accessed | tf_op | source)
XLA Modules:
  0.0 136.7 jit_solution(11342812192215976992)
XLA Ops:
  7.2 0.8 fusion
  8.0 0.1 copy.11
  8.1 0.9 broadcast_in_dim.2
  8.9 7.7 %all-to-all-start = ((bf16[8,256,128]{2,1,0:T(8,128)(2,1)}), bf16[8,256,128]{2,1,0:T(8,128)(2,1)S(1)}, u32[]{:S(2)}, u32[]{:S(2)}) async-start(bf16[8,256,128]{2,1,0:T(8,128)(2,1)} %broadcast_in_dim.2), calls=%async_computation | async-start | bytes 1048576 | tf_op jit(solution)/shard_map/all_to_all | solution.py:55
  16.6 0.0 all-gather.3.cloned.1.call-start
  16.6 1.4 %pad_maximum_fusion.2 = f32[32,512]{1,0:T(8,128)} fusion(f32[8,512]{1,0:T(8,128)} %slopes.1, f32[8,512]{1,0:T(8,128)} %steps.1), kind=kLoop, calls=%fused_computation.2 | loop fusion | flops 49152 | bytes 98304 | tf_op jit(solution)/shard_map/concatenate | solution.py:323
  18.1 0.0 all-gather.3.cloned.1.call-update
  18.1 4.5 %pad_maximum_fusion.t = bf16[128,16384]{1,0:T(8,128)(2,1)} fusion(bf16[64,16384]{1,0:T(8,128)(2,1)} %bitcast.13), kind=kLoop, calls=%fused_computation | loop fusion | flops 8388608 | bytes 6291456 | tf_op jit(solution)/shard_map/concatenate | solution.py:305
  22.6 0.0 copy-start
  22.6 2.2 %copy-done = bf16[128,16384]{1,0:T(8,128)(2,1)S(1)} copy-done((bf16[128,16384]{1,0:T(8,128)(2,1)S(1)}, bf16[128,16384]{1,0:T(8,128)(2,1)}, u32[]{:S(2)}) %copy-start) | copy-done | bytes 4194328
  24.8 0.0 copy-start.11
  24.8 0.0 copy-start.9
  24.8 0.0 copy-start.10
  24.8 3.0 %shard_map.95.t = bf16[16384,128]{1,0:T(8,128)(2,1)S(1)} custom-call(bf16[128,16384]{1,0:T(8,128)(2,1)S(1)} %copy-done), custom_call_target="tpu_custom_call" | custom-call | tf_op jit(solution)/shard_map/pallas_call | solution.py:320
  27.8 0.0 copy-start.2
  27.8 2.0 %copy-done.2 = bf16[16384,128]{1,0:T(8,128)(2,1)} copy-done((bf16[16384,128]{1,0:T(8,128)(2,1)}, bf16[16384,128]{1,0:T(8,128)(2,1)S(1)}, u32[]{:S(2)}) %copy-start.2) | copy-done | bytes 4194328
  29.8 0.0 copy-done.11
  29.8 0.1 copy.10.block_map
  29.9 1.4 %all-to-all-done.mine = bf16[8,256,128]{2,1,0:T(8,128)(2,1)S(1)} async-done(((bf16[8,256,128]{2,1,0:T(8,128)(2,1)}), bf16[8,256,128]{2,1,0:T(8,128)(2,1)S(1)}, u32[]{:S(2)}, u32[]{:S(2)}) %all-to-all-start) | async-done | bytes 524320 | tf_op jit(solution)/shard_map/all_to_all | solution.py:55
  31.3 5.6 %collective-permute-start = (bf16[8,256,128]{2,1,0:T(8,128)(2,1)S(1)}, bf16[8,256,128]{2,1,0:T(8,128)(2,1)S(1)}, u32[]{:S(2)}, u32[]{:S(2)}) collective-permute-start(bf16[8,256,128]{2,1,0:T(8,128)(2,1)S(1)} %all-to-all-done.mine), channel_id=1, source_target_pairs={{0,1},{1,0},{2,3},{3,2},{4,5},{5,4},{6,7},{7,6},{8,9},{9,8},{10,11... | collective-permute-start | bytes 1572872 | tf_op jit(solution)/shard_map/ppermute | solution.py:321
  36.9 0.1 pad_add_fusion.rank
  37.0 0.0 copy-done.9
  37.0 4.4 %shard_map.94 = (s32[642]{0:T(1024)S(1)}, s32[642]{0:T(1024)S(1)}, s32[1]{0:T(128)}) custom-call(s32[2]{0:T(128)S(1)} %pad_add_fusion.rank, s32[32,20]{1,0:T(8,128)S(1)} %copy.10.block_map, s32[32]{0:T(128)S(1)} %copy-done.9), custom_call_target="tpu_custom_call" | custom-call | tf_op jit(solution)/shard_map/pallas_call | solution.py:313
  41.4 0.1 compare_convert_fusion.mask
  41.5 0.0 collective-permute-done.other
  41.5 0.0 copy-done.10
  41.5 0.0 copy-start.1
  41.5 2.2 %copy-done.1 = bf16[128,16384]{1,0:T(8,128)(2,1)S(1)} copy-done((bf16[128,16384]{1,0:T(8,128)(2,1)S(1)}, bf16[128,16384]{1,0:T(8,128)(2,1)}, u32[]{:S(2)}) %copy-start.1) | copy-done | bytes 4194328
  43.7 7.8 %shard_map.96 = (f32[32,4,128]{2,1,0:T(4,128)S(1)}, bf16[32,256,128]{2,1,0:T(8,128)(2,1)S(1)}) custom-call(s32[2]{0:T(128)S(1)} %pad_add_fusion.rank, s32[642]{0:T(1024)S(1)} %get-tuple-element.14.src, s32[642]{0:T(1024)S(1)} %get-tuple-element.15.tgt, s32[1]{0:T(128)} %get-tuple-element.16.total, bf16[8,256,128]{2,1,0:T(8,128)(2,1)S(1)} %all-to-all-done.mine, ...), custom_call_target="tpu_custom_call" | custom-call | flops 10000000000 | bytes 20000000 | tf_op jit(solution)/shard_map/pallas_call | solution.py:326
  51.5 21.6 %all_to_all.25.arrived = f32[32,4,128]{2,1,0:T(4,128)S(1)} all-to-all(f32[32,4,128]{2,1,0:T(4,128)S(1)} %get-tuple-element.22), channel_id=1, replica_groups=mesh['src_0'=4,'src_1'=8,'tgt_0'=8,'tgt_1'=2] {'src_0','src_1'}, dimensions={0} | all-to-all | bytes 131072 | tf_op jit(solution)/shard_map/all_to_all | solution.py:55
  73.0 0.1 shard_map.97
  73.1 12.1 %all_to_all.26.level = f32[32,4,128]{2,1,0:T(4,128)S(1)} all-to-all(f32[32,4,128]{2,1,0:T(4,128)S(1)} %shard_map.97), channel_id=1, replica_groups=mesh['src_0'=4,'src_1'=8,'tgt_0'=8,'tgt_1'=2] {'src_0','src_1'}, dimensions={0} | all-to-all | bytes 131072 | tf_op jit(solution)/shard_map/all_to_all | solution.py:55
  85.2 0.0 all-gather.3.cloned.1.call-done
  85.2 0.0 copy-start.3
  85.2 2.2 %copy-done.3 = bf16[16384,128]{1,0:T(8,128)(2,1)S(1)} copy-done((bf16[16384,128]{1,0:T(8,128)(2,1)S(1)}, bf16[16384,128]{1,0:T(8,128)(2,1)}, u32[]{:S(2)}) %copy-start.3) | copy-done | bytes 4194328
  87.4 0.0 copy-start.4
  87.4 1.2 copy-done.4
  88.6 0.0 copy-start.5
  88.6 0.0 copy-start.6
  88.6 0.0 copy-start.7
  88.6 7.0 %shard_map.98 = f32[16,8,128]{2,1,0:T(8,128)} custom-call(s32[642]{0:T(1024)S(1)} %get-tuple-element.14.src, s32[642]{0:T(1024)S(1)} %get-tuple-element.15.tgt, s32[1]{0:T(128)} %get-tuple-element.16.total, bf16[32,256,128]{2,1,0:T(8,128)(2,1)S(1)} %get-tuple-element.20.x, bf16[16384,128]{1,0:T(8,128)(2,1)S(1)} %copy-done.3, f32[64,128]{1,0:T(8,128)S(1)} %bitcast.12, ...), custom_call_target="tpu_custom_call" | custom-call | flops 10000000000 | bytes 20000000 | tf_op jit(solution)/shard_map/pallas_call | solution.py:355
  95.6 8.5 %all-to-all-start.3 = ((f32[16,8,128]{2,1,0:T(8,128)}), f32[16,8,128]{2,1,0:T(8,128)S(1)}, u32[]{:S(2)}, u32[]{:S(2)}) async-start(f32[16,8,128]{2,1,0:T(8,128)} %shard_map.98), calls=%async_computation.3 | async-start | bytes 131072 | tf_op jit(solution)/shard_map/all_to_all | solution.py:55
  104.1 0.0 copy-done.5
  104.1 0.9 shard_map.99.moments
  105.0 6.9 %all-to-all-done.3.arrived = f32[16,8,128]{2,1,0:T(8,128)S(1)} async-done(((f32[16,8,128]{2,1,0:T(8,128)}), f32[16,8,128]{2,1,0:T(8,128)S(1)}, u32[]{:S(2)}, u32[]{:S(2)}) %all-to-all-start.3) | async-done | bytes 65568 | tf_op jit(solution)/shard_map/all_to_all | solution.py:55
  111.9 0.6 shard_map.100
  112.6 7.1 %all-to-all-start.4 = ((f32[32,1,128]{2,1,0:T(1,128)}), f32[32,1,128]{2,1,0:T(1,128)S(1)}, u32[]{:S(2)}, u32[]{:S(2)}) async-start(f32[32,1,128]{2,1,0:T(1,128)} %get-tuple-element.24), calls=%async_computation.4 | async-start | bytes 32768 | tf_op jit(solution)/shard_map/all_to_all | solution.py:55
  119.6 0.6 broadcast_multiply_fusion
  120.3 8.0 %all-to-all-done.4.arrived = f32[32,1,128]{2,1,0:T(1,128)S(1)} async-done(((f32[32,1,128]{2,1,0:T(1,128)}), f32[32,1,128]{2,1,0:T(1,128)S(1)}, u32[]{:S(2)}, u32[]{:S(2)}) %all-to-all-start.4) | async-done | bytes 16416 | tf_op jit(solution)/shard_map/all_to_all | solution.py:55
  128.3 0.0 copy-done.6
  128.3 0.0 copy-done.7
  128.3 0.0 copy-start.8
  128.3 0.7 copy-done.8
  129.0 0.9 shard_map.101
  (3 shorter events, 0.0 us)
Async XLA Ops:
  8.9 22.4 %all-to-all-start = ((bf16[8,256,128]{2,1,0:T(8,128)(2,1)}), bf16[8,256,128]{2,1,0:T(8,128)(2,1)S(1)}, u32[]{:S(2)}, u32[]{:S(2)}) async-start(bf16[8,256,128]{2,1,0:T(8,128)(2,1)} %broadcast_in_dim.2), calls=%async_computation | async-start | bytes 1048576 | tf_op jit(solution)/shard_map/all_to_all | solution.py:55
  16.6 68.6 %all-gather.3.cloned.1.call-start = ((), (), s32[]{:S(2)}) async-start(), calls=%async_computation.5 | async-start | bytes 1114112 | tf_op jit(solution)/shard_map/all_gather | solution.py:324
  22.6 2.2 %copy-start = (bf16[128,16384]{1,0:T(8,128)(2,1)S(1)}, bf16[128,16384]{1,0:T(8,128)(2,1)}, u32[]{:S(2)}) copy-start(bf16[128,16384]{1,0:T(8,128)(2,1)} %pad_maximum_fusion.t) | copy-start | bytes 12582916
  24.8 5.0 %copy-start.11 = (s32[32,20]{0,1:T(8,128)S(1)}, s32[32,20]{0,1:T(8,128)}, u32[]{:S(2)}) copy-start(s32[32,20]{0,1:T(8,128)} %param.10) | copy-start | bytes 7684
  24.8 12.2 %copy-start.9 = (s32[32]{0:T(128)S(1)}, s32[32]{0:T(128)}, u32[]{:S(2)}) copy-start(s32[32]{0:T(128)} %counts.1) | copy-start | bytes 388
  24.8 16.7 %copy-start.10 = (f32[8192]{0:T(1024)S(1)}, f32[8192]{0:T(1024)}, u32[]{:S(2)}) copy-start(f32[8192]{0:T(1024)} %param.9) | copy-start | bytes 98308
  27.8 2.0 %copy-start.2 = (bf16[16384,128]{1,0:T(8,128)(2,1)}, bf16[16384,128]{1,0:T(8,128)(2,1)S(1)}, u32[]{:S(2)}) copy-start(bf16[16384,128]{1,0:T(8,128)(2,1)S(1)} %shard_map.95.t) | copy-start | bytes 12582916
  31.3 10.2 %collective-permute-start = (bf16[8,256,128]{2,1,0:T(8,128)(2,1)S(1)}, bf16[8,256,128]{2,1,0:T(8,128)(2,1)S(1)}, u32[]{:S(2)}, u32[]{:S(2)}) collective-permute-start(bf16[8,256,128]{2,1,0:T(8,128)(2,1)S(1)} %all-to-all-done.mine), channel_id=1, source_target_pairs={{0,1},{1,0},{2,3},{3,2},{4,5},{5,4},{6,7},{7,6},{8,9},{9,8},{10,11... | collective-permute-start | bytes 1572872 | tf_op jit(solution)/shard_map/ppermute | solution.py:321
  41.5 2.2 %copy-start.1 = (bf16[128,16384]{1,0:T(8,128)(2,1)S(1)}, bf16[128,16384]{1,0:T(8,128)(2,1)}, u32[]{:S(2)}) copy-start(bf16[128,16384]{1,0:T(8,128)(2,1)} %pad_maximum_fusion.t) | copy-start | bytes 12582916
  85.2 2.2 %copy-start.3 = (bf16[16384,128]{1,0:T(8,128)(2,1)S(1)}, bf16[16384,128]{1,0:T(8,128)(2,1)}, u32[]{:S(2)}) copy-start(bf16[16384,128]{1,0:T(8,128)(2,1)} %copy-done.2) | copy-start | bytes 12582916
  87.4 1.2 copy-start.4
  88.6 15.5 %copy-start.5 = (f32[512,512]{1,0:T(8,128)S(1)}, f32[512,512]{1,0:T(8,128)}, u32[]{:S(2)}) copy-start(f32[512,512]{1,0:T(8,128)} %all-gather.3.cloned.1.call-done) | copy-start | bytes 3145732
  88.6 39.7 %copy-start.6 = (f32[8,512]{1,0:T(8,128)S(1)}, f32[8,512]{1,0:T(8,128)}, u32[]{:S(2)}) copy-start(f32[8,512]{1,0:T(8,128)} %slopes.1) | copy-start | bytes 49156
  88.6 39.7 %copy-start.7 = (f32[8,512]{1,0:T(8,128)S(1)}, f32[8,512]{1,0:T(8,128)}, u32[]{:S(2)}) copy-start(f32[8,512]{1,0:T(8,128)} %steps.1) | copy-start | bytes 49156
  95.6 16.3 %all-to-all-start.3 = ((f32[16,8,128]{2,1,0:T(8,128)}), f32[16,8,128]{2,1,0:T(8,128)S(1)}, u32[]{:S(2)}, u32[]{:S(2)}) async-start(f32[16,8,128]{2,1,0:T(8,128)} %shard_map.98), calls=%async_computation.3 | async-start | bytes 131072 | tf_op jit(solution)/shard_map/all_to_all | solution.py:55
  112.6 15.7 %all-to-all-start.4 = ((f32[32,1,128]{2,1,0:T(1,128)}), f32[32,1,128]{2,1,0:T(1,128)S(1)}, u32[]{:S(2)}, u32[]{:S(2)}) async-start(f32[32,1,128]{2,1,0:T(1,128)} %get-tuple-element.24), calls=%async_computation.4 | async-start | bytes 32768 | tf_op jit(solution)/shard_map/all_to_all | solution.py:55
  128.3 0.7 copy-start.8
Sparse Core Ops, SparseCore 0:
  20.1 46.2 all-gather.2

commit v2 on v1

--- a/solution.py
+++ b/solution.py
@@ -18,7 +18,8 @@
 LN2 = 0.6931471805599453
 entropy = 0.5
 SCALE = LOG2E / entropy
-UNROLL = 2
+UNROLL = 8
+WIDE = 64
 F32 = jnp.float32
 
 VMEM = pl.BlockSpec(memory_space=pltpu.VMEM)
@@ -79,23 +80,57 @@
         tgt[n + extra] = own_blocks
 
 
-def lay_out(rank, mine, other, mask, rows):
+def split_three(value):
+    high = value.astype(jnp.bfloat16).astype(F32)
+    rest = value - high
+    middle = rest.astype(jnp.bfloat16).astype(F32)
+    return high, middle, rest - middle
+
+
+def columns_kernel(pot, out):
+    row = lax.broadcasted_iota(jnp.int32, (HALF, HALF), 0)
+    ones = jnp.where((row >= WIDE + 3) & (row < WIDE + 6), 1.0, 0.0)
+
+    def turn(c, carry):
+        parts = split_three(pot[pl.ds(c, 1), :])
+        tile = ones
+        for k in range(3):
+            tile = jnp.where(row == WIDE + k, parts[k], tile)
+        at = pl.ds(pl.multiple_of(lax.rem(c, 2) * HALF, HALF), HALF)
+        out[lax.shift_right_logical(c, 1), at, :] = jnp.transpose(tile).astype(jnp.bfloat16)
+        return carry
+
+    lax.fori_loop(0, pot.shape[0], turn, 0, unroll=4)
+
+
+def lay_out(rank, mine, other, columns, x):
     core = rank[1]
+    lane = lax.broadcasted_iota(jnp.int32, (BLOCK, HALF), 1)
     for arrived, side in ((mine, core), (other, 1 - core)):
         for y in range(arrived.shape[0]):
-            piece = arrived[y].reshape(BLOCK // 16, 16, HALF)
+            piece = arrived[y]
             for half in range(2):
-                lanes = mask[half * 16 : half * 16 + 16, :]
-                rows[4 * y + 2 * side + half] = (piece * lanes[None]).reshape(BLOCK, HALF)
+                b = 4 * y + 2 * side + half
+                if half:
+                    piece = jnp.concatenate([piece[:, WIDE:], piece[:, :WIDE]], axis=1)
+                x[b] = jnp.where(lane < WIDE, piece, columns[b])
+
+
+def target_columns(t, tb, h, extra):
+    cols = t[:, pl.ds(pl.multiple_of(tb * BLOCK + h * HALF, HALF), HALF)]
+    zeros = jnp.zeros((HALF - WIDE - 16, HALF), jnp.bfloat16)
+    return jnp.concatenate([cols, extra.astype(jnp.bfloat16), zeros], axis=0)
 
 
 def column_kernel(
-    blocks, own_blocks, rank, src, tgt, total, mine, other, t, pot, mask, out, x, peak, acc
+    blocks, own_blocks, rank, src, tgt, total, mine, other, t, columns, out, x, peak, acc
 ):
-    lay_out(rank, mine, other, mask, x)
+    lay_out(rank, mine, other, columns, x)
     peak[...] = jnp.full(peak.shape, NEG, F32)
     acc[...] = jnp.zeros(acc.shape, F32)
     live = total[0]
+    row = lax.broadcasted_iota(jnp.int32, (16, HALF), 0)
+    extra = jnp.where(row < 3, 1.0, 0.0)
 
     def turn(step, carry):
         found = []
@@ -105,14 +140,8 @@
             b = jnp.minimum(b_all, blocks - 1)
             tb = jnp.minimum(t_all, own_blocks - 1)
             rows = x[b]
-            pieces = []
             for h in range(2):
-                line = pot[pl.ds(2 * b + h, 1), :] * SCALE
-                pieces.append(jnp.transpose(jnp.broadcast_to(line, (HALF, HALF))))
-            shift = jnp.concatenate(pieces, axis=0)
-            for h in range(2):
-                cols = t[:, pl.ds(pl.multiple_of(tb * BLOCK + h * HALF, HALF), HALF)]
-                s = nn(rows, cols) * SCALE + shift
+                s = nn(rows, target_columns(t, tb, h, extra)) * SCALE
                 s = s.reshape(BLOCK // 8, 8, HALF)
                 top = jnp.max(s, axis=0)
                 part = jnp.sum(jnp.exp2(s - top[None]), axis=0)
@@ -150,18 +179,9 @@
     whole = jnp.zeros_like(top)
     for p in range(peers):
         whole = whole + jnp.exp2(arrived[p] - top)
-    level = top + jnp.log2(whole)
+    level = (-entropy * LN2) * (top + jnp.log2(whole))
     for p in range(peers):
         out[p] = level
-
-
-def turn_kernel(t, out):
-    def turn(c, carry):
-        at = pl.ds(pl.multiple_of(c * HALF, HALF), HALF)
-        out[at, :] = jnp.transpose(t[:, at])
-        return carry
-
-    lax.fori_loop(0, t.shape[1] // HALF, turn, 0, unroll=4)
 
 
 def moments_kernel(peers, stored, pairs, out, square):
@@ -182,10 +202,12 @@
 
 
 def row_kernel(
-    blocks, own_blocks, ratio, peers, src, tgt, total, x, t, pot, level, pairs, out, acc
+    blocks, own_blocks, ratio, peers, src, tgt, total, x, t, level, pairs, out, acc, sums
 ):
     acc[...] = jnp.zeros(acc.shape, F32)
     live = total[0]
+    row = lax.broadcasted_iota(jnp.int32, (16, HALF), 0)
+    ones = jnp.where(row < 3, 1.0, 0.0)
 
     def turn(step, carry):
         found = []
@@ -195,40 +217,42 @@
             b = jnp.minimum(b_all, blocks - 1)
             tb = jnp.minimum(t_all, own_blocks - 1)
             rows = x[b]
-            lines = [pot[pl.ds(2 * b + h, 1), :] * SCALE for h in range(2)]
-            line = jnp.concatenate(lines, axis=1)
             parts = None
             for h in range(2):
-                cols = t[pl.ds(pl.multiple_of(tb * BLOCK + h * HALF, HALF), HALF), :]
-                log_line = level[
+                line = level[
                     lax.shift_right_logical(tb, 1), pl.ds(lax.rem(tb, 2) * 2 + h, 1), :
                 ]
-                shift = jnp.transpose(jnp.broadcast_to(log_line, (HALF, HALF)))
-                s = nt(cols, rows) * SCALE + line
-                e = jnp.exp2(s - jnp.concatenate([shift, shift], axis=1))
-                part = jnp.sum(e.reshape(HALF // 8, 8, BLOCK), axis=0)
-                parts = part if parts is None else parts + part
+                extra = ones
+                for k, part in enumerate(split_three(line)):
+                    extra = jnp.where(row == 3 + k, part, extra)
+                e = jnp.exp2(nn(rows, target_columns(t, tb, h, extra)) * SCALE)
+                parts = e if parts is None else parts + e
             found.append((b_all, parts))
         for b_all, parts in found:
-            at = pl.ds(pl.multiple_of(b_all * 8, 8), 8)
-            acc[at, :] = acc[at, :] + parts
+            acc[b_all] = acc[b_all] + parts
         return carry
 
     lax.fori_loop(0, (live + UNROLL - 1) // UNROLL, turn, 0)
+
+    def fold(b, carry):
+        for h in range(2):
+            turned = jnp.transpose(acc[b, h * HALF : (h + 1) * HALF, :])
+            at = pl.ds(lax.rem(b, 2) * 2 + h, 1)
+            sums[lax.shift_right_logical(b, 1), at, :] = jnp.sum(turned, axis=0, keepdims=True)
+        return carry
+
+    lax.fori_loop(0, blocks, fold, 0, unroll=4)
 
     rows_kept = pairs.shape[1] // 2
     lane = lax.broadcasted_iota(jnp.int32, (rows_kept, HALF), 1)
     row = lax.broadcasted_iota(jnp.int32, (rows_kept, HALF), 0)
     dots = jnp.zeros((rows_kept, HALF), F32)
     for p in range(blocks // 2):
-        for half in range(2):
-            at = pl.ds((2 * p + half) * 8, 8)
-            part = 1.0 / peers - ratio * jnp.sum(acc[at, :], axis=0, keepdims=True)
-            for h in range(2):
-                q = 2 * half + h
-                line = part[:, h * HALF : (h + 1) * HALF]
-                out[p, q : q + 1, :] = line
-                dots = dots + pairs[p, :rows_kept, q * HALF : (q + 1) * HALF] * line
+        part = 1.0 / peers - ratio * sums[p]
+        out[p, :4, :] = part
+        for q in range(4):
+            at = slice(q * HALF, (q + 1) * HALF)
+            dots = dots + pairs[p, :rows_kept, at] * part[q : q + 1]
     spread = jnp.where(lane == row, jnp.sum(dots, axis=1, keepdims=True), 0.0)
     value = jnp.sum(spread, axis=0, keepdims=True)
     for p in range(blocks // 2):
@@ -301,12 +325,10 @@
     packed = jnp.concatenate([sources[:BLOCK], sources[BLOCK:]], axis=1)
     mine = share(packed, TGT[0])
     core = lax.axis_index(TGT[1])
-    ttt = targets.T
-    t = jnp.concatenate([ttt, ttt], axis=0)
-    pot = potential.reshape(-1, HALF)
-    lane = jnp.arange(HALF, dtype=jnp.int32)[None, :] // 64
-    mask_row = jnp.arange(32, dtype=jnp.int32)[:, None] // 16
-    mask = (lane == mask_row).astype(jnp.bfloat16)
+    t = targets.T
+    columns = call(
+        columns_kernel, sds((blocks, BLOCK, HALF), jnp.bfloat16), [VMEM], VMEM
+    )(potential.reshape(-1, HALF))
 
     rank = jnp.stack([lax.axis_index(TGT), core]).astype(jnp.int32)
     slots = blocks * listed + UNROLL
@@ -317,20 +339,19 @@
         [SMEM] * 3,
     )(rank, block_map, counts)
 
-    turned = call(turn_kernel, sds((targets.shape[0], HALF), jnp.bfloat16), [VMEM], VMEM)(t)
+    mine, columns, src, tgt, total = lax.optimization_barrier((mine, columns, src, tgt, total))
     other = lax.ppermute(mine, TGT[1], [(0, 1), (1, 0)])
-    mine, other, t, turned = lax.optimization_barrier((mine, other, t, turned))
     history = jnp.concatenate([step_history, slope_history] * 2, axis=0)
     pairs = lax.all_gather(history, TGT)
 
     levels, x = call(
         functools.partial(column_kernel, blocks, own_blocks),
         (sds((src_size, 4, HALF)), sds((blocks, BLOCK, HALF), jnp.bfloat16)),
-        [SMEM] * 4 + [VMEM] * 5,
+        [SMEM] * 4 + [VMEM] * 4,
         [VMEM] * 2,
         [pltpu.VMEM((8 * own_blocks + 8, BLOCK), F32)] * 2,
         pl.CostEstimate(flops=10**10, bytes_accessed=2 * 10**7, transcendentals=4 * 10**6),
-    )(rank, src, tgt, total, mine, other, t, pot, mask)
+    )(rank, src, tgt, total, mine, other, t, columns)
 
     arrived = swap(levels, SRC)
 
@@ -341,7 +362,7 @@
         VMEM,
     )(arrived)
     level = swap(level, SRC)
-    target_potential = (-entropy * LN2) * level.reshape(-1)
+    target_potential = level.reshape(-1)
 
     moments = call(
         functools.partial(moments_kernel, tgt_size, stored),
@@ -355,11 +376,11 @@
     parts = call(
         functools.partial(row_kernel, blocks, own_blocks, ratio, tgt_size),
         sds((tgt_size, 8, HALF)),
-        [SMEM] * 3 + [VMEM] * 5,
+        [SMEM] * 3 + [VMEM] * 4,
         VMEM,
-        [pltpu.VMEM((8 * blocks + 8, BLOCK), F32)],
+        [pltpu.VMEM((blocks + 1, BLOCK, HALF), F32), pltpu.VMEM((tgt_size, 4, HALF), F32)],
         pl.CostEstimate(flops=10**10, bytes_accessed=2 * 10**7, transcendentals=4 * 10**6),
-    )(src, tgt, total, x, turned, pot, level, pairs)
+    )(src, tgt, total, x, t, level, pairs)
 
     gradient, dots = call(
         functools.partial(gradient_kernel, tgt_size, src_size),

time: 137 us -> 131 us (0.956)
  waiting for transfers between devices: 16.3 us -> 24 us
  other arithmetic: 6.78 us -> 1.51 us
  Pallas kernels: 24.6 us -> 19.6 us
  starting transfers between devices: 28.8 us -> 26.7 us
  local copies, waits for them, and re-layouts: 12.3 us -> 10.6 us
    all_to_all x3, waiting for transfers between devices: 16.3 us -> 22.4 us  [swap(): return lax.all_to_all(x, axis, 0, 0, tiled=True)]
    concatenate x1 -> x0, other arithmetic: 4.54 us -> none  [per_device(): t = jnp.concatenate([ttt, ttt], axis=0)]
    pallas_call x1, Pallas kernels: 7.75 us -> 5.06 us  [per_device(): call(functools.partial(column_kernel, blocks, own_blocks), (sds((src_size...]
    all_to_all x3, starting transfers between devices: 23.2 us -> 21.1 us  [swap(): return lax.all_to_all(x, axis, 0, 0, tiled=True)]
    unnamed x25 -> x26, local copies, waits for them, and re-layouts: 10.6 us -> 8.79 us
    ppermute x1, waiting for transfers between devices: 0.01 us -> 1.51 us  [per_device(): other = lax.ppermute(mine, TGT[1], [(0, 1), (1, 0)])]
  transfers between devices with their start and end apart: 5 -> 5, of which waited for: 3 -> 4; matrix products, arithmetic and copies ran while one was open for 5% -> 1% of each run, Pallas kernels for 12% -> 9%
where the time goes in v2:
time: 131 us; the launch traced here: 130 us
  blocking collectives  33.5 us (26%)
  starting transfers between devices  26.7 us (20%)
  waiting for transfers between devices  24 us (18%)
  Pallas kernels  19.6 us (15%)
  between operations  14.2 us (11%)
  local copies, waits for them, and re-layouts  10.6 us (8%)
  other arithmetic  1.51 us (1%)
    all_to_all x2, blocking collectives, swap(): return lax.all_to_all(x, axis, 0, 0, tiled=True)  33.5 us
    all_to_all x3, waiting for transfers between devices, swap(): return lax.all_to_all(x, axis, 0, 0, tiled=True)  22.4 us
    all_to_all x3, starting transfers between devices, swap(): return lax.all_to_all(x, axis, 0, 0, tiled=True)  21.1 us
    unnamed x26, local copies, waits for them, and re-layouts  8.79 us
    pallas_call x1, Pallas kernels, per_device(): call(functools.partial(row_kernel, blocks, own_blocks, ratio, tgt_size),...  5.92 us
    ppermute x1, starting transfers between devices, per_device(): other = lax.ppermute(mine, TGT[1], [(0, 1), (1, 0)])  5.59 us
    pallas_call x1, Pallas kernels, per_device(): call(functools.partial(column_kernel, blocks, own_blocks), (sds((src_size...  5.06 us
    pallas_call x1, Pallas kernels, per_device(): call(functools.partial(listing_kernel, blocks, own_blocks), (sds((slots,)...  4.37 us
  transfers between devices with their start and end apart: 5, of which 4 were waited for; matrix products, arithmetic and copies ran while one was open for 1% of the time, Pallas kernels for 9%

profile of v2, /device:TPU:1, one launch (start us, length us, event | category | flops | bytes accessed | tf_op | source)
XLA Modules:
  0.0 130.0 jit_solution(10218714466433933017)
XLA Ops:
  7.2 0.0 copy-start.11
  7.2 0.0 copy-start.4
  7.2 0.8 fusion
  8.0 0.0 copy-start.6
  8.0 0.1 copy.10
  8.1 0.9 broadcast_in_dim.2
  9.0 7.7 %all-to-all-start = ((bf16[8,256,128]{2,1,0:T(8,128)(2,1)}), bf16[8,256,128]{2,1,0:T(8,128)(2,1)S(1)}, u32[]{:S(2)}, u32[]{:S(2)}) async-start(bf16[8,256,128]{2,1,0:T(8,128)(2,1)} %broadcast_in_dim.2), calls=%async_computation | async-start | bytes 1048576 | tf_op jit(solution)/shard_map/all_to_all | solution.py:56
  16.6 0.0 all-gather.3.cloned.1.call-start
  16.7 1.4 %pad_maximum_fusion.1 = f32[32,512]{1,0:T(8,128)} fusion(f32[8,512]{1,0:T(8,128)} %slopes.1, f32[8,512]{1,0:T(8,128)} %steps.1), kind=kLoop, calls=%fused_computation.1 | loop fusion | flops 49152 | bytes 98304 | tf_op jit(solution)/shard_map/concatenate | solution.py:344
  18.1 0.0 all-gather.3.cloned.1.call-update
  18.1 0.0 copy-done.11
  18.1 0.1 copy.11.block_map
  18.2 0.0 copy-done.4
  18.2 1.7 %shard_map.94.columns = bf16[32,256,128]{2,1,0:T(8,128)(2,1)S(1)} custom-call(f32[64,128]{1,0:T(8,128)S(1)} %bitcast.11), custom_call_target="tpu_custom_call" | custom-call | tf_op jit(solution)/shard_map/pallas_call | solution.py:329
  20.0 0.1 pad_add_fusion.rank
  20.1 0.0 copy-done.6
  20.1 4.4 %shard_map.95 = (s32[648]{0:T(1024)S(1)}, s32[648]{0:T(1024)S(1)}, s32[1]{0:T(128)}) custom-call(s32[2]{0:T(128)S(1)} %pad_add_fusion.rank, s32[32,20]{1,0:T(8,128)S(1)} %copy.11.block_map, s32[32]{0:T(128)S(1)} %copy-done.6), custom_call_target="tpu_custom_call" | custom-call | tf_op jit(solution)/shard_map/pallas_call | solution.py:335
  24.4 6.9 %all-to-all-done.mine = bf16[8,256,128]{2,1,0:T(8,128)(2,1)S(1)} async-done(((bf16[8,256,128]{2,1,0:T(8,128)(2,1)}), bf16[8,256,128]{2,1,0:T(8,128)(2,1)S(1)}, u32[]{:S(2)}, u32[]{:S(2)}) %all-to-all-start) | async-done | bytes 524320 | tf_op jit(solution)/shard_map/all_to_all | solution.py:56
  31.4 5.6 %collective-permute-start = (bf16[8,256,128]{2,1,0:T(8,128)(2,1)S(1)}, bf16[8,256,128]{2,1,0:T(8,128)(2,1)S(1)}, u32[]{:S(2)}, u32[]{:S(2)}) collective-permute-start(bf16[8,256,128]{2,1,0:T(8,128)(2,1)S(1)} %all-to-all-done.mine), channel_id=1, source_target_pairs={{0,1},{1,0},{2,3},{3,2},{4,5},{5,4},{6,7},{7,6},{8,9},{9,8},{10,11... | collective-permute-start | bytes 1572872 | tf_op jit(solution)/shard_map/ppermute | solution.py:343
  37.0 1.5 %collective-permute-done.other = bf16[8,256,128]{2,1,0:T(8,128)(2,1)S(1)} collective-permute-done((bf16[8,256,128]{2,1,0:T(8,128)(2,1)S(1)}, bf16[8,256,128]{2,1,0:T(8,128)(2,1)S(1)}, u32[]{:S(2)}, u32[]{:S(2)}) %collective-permute-start) | collective-permute-done | bytes 524320 | tf_op jit(solution)/shard_map/ppermute | solution.py:343
  38.5 0.0 copy-start.7
  38.5 1.6 %copy-done.7 = bf16[16384,64]{0,1:T(8,128)(2,1)S(1)} copy-done((bf16[16384,64]{0,1:T(8,128)(2,1)S(1)}, bf16[16384,64]{0,1:T(8,128)(2,1)}, u32[]{:S(2)}) %copy-start.7) | copy-done | bytes 2097176
  40.1 5.1 %shard_map.96 = (f32[32,4,128]{2,1,0:T(4,128)S(1)}, bf16[32,256,128]{2,1,0:T(8,128)(2,1)S(1)}) custom-call(s32[2]{0:T(128)S(1)} %pad_add_fusion.rank, s32[648]{0:T(1024)S(1)} %get-tuple-element.18.src, s32[648]{0:T(1024)S(1)} %get-tuple-element.19.tgt, s32[1]{0:T(128)} %get-tuple-element.20.total, bf16[8,256,128]{2,1,0:T(8,128)(2,1)S(1)} %all-to-all-done.mine, ...), custom_call_target="tpu_custom_call" | custom-call | flops 10000000000 | bytes 20000000 | tf_op jit(solution)/shard_map/pallas_call | solution.py:347
  45.2 0.0 copy-start.9
  45.2 1.3 %copy-done.9 = bf16[32,256,128]{2,1,0:T(8,128)(2,1)} copy-done((bf16[32,256,128]{2,1,0:T(8,128)(2,1)}, bf16[32,256,128]{2,1,0:T(8,128)(2,1)S(1)}, u32[]{:S(2)}) %copy-start.9) | copy-done | bytes 2097176
  46.5 21.5 %all_to_all.25.arrived = f32[32,4,128]{2,1,0:T(4,128)S(1)} all-to-all(f32[32,4,128]{2,1,0:T(4,128)S(1)} %get-tuple-element.24), channel_id=1, replica_groups=mesh['src_0'=4,'src_1'=8,'tgt_0'=8,'tgt_1'=2] {'src_0','src_1'}, dimensions={0} | all-to-all | bytes 131072 | tf_op jit(solution)/shard_map/all_to_all | solution.py:56
  68.1 0.1 shard_map.97
  68.2 12.0 %all_to_all.26.level = f32[32,4,128]{2,1,0:T(4,128)S(1)} all-to-all(f32[32,4,128]{2,1,0:T(4,128)S(1)} %shard_map.97), channel_id=1, replica_groups=mesh['src_0'=4,'src_1'=8,'tgt_0'=8,'tgt_1'=2] {'src_0','src_1'}, dimensions={0} | all-to-all | bytes 131072 | tf_op jit(solution)/shard_map/all_to_all | solution.py:56
  80.2 0.0 all-gather.3.cloned.1.call-done
  80.2 0.0 copy-start
  80.2 1.2 copy-done
  81.4 0.0 copy-start.8
  81.4 1.6 %copy-done.8 = bf16[16384,64]{0,1:T(8,128)(2,1)S(1)} copy-done((bf16[16384,64]{0,1:T(8,128)(2,1)S(1)}, bf16[16384,64]{0,1:T(8,128)(2,1)}, u32[]{:S(2)}) %copy-start.8) | copy-done | bytes 2097176
  83.0 0.0 copy-start.10
  83.0 1.6 %copy-done.10 = bf16[32,256,128]{2,1,0:T(8,128)(2,1)S(1)} copy-done((bf16[32,256,128]{2,1,0:T(8,128)(2,1)S(1)}, bf16[32,256,128]{2,1,0:T(8,128)(2,1)}, u32[]{:S(2)}) %copy-start.10) | copy-done | bytes 2097176
  84.6 0.0 copy-start.1
  84.6 0.0 copy-start.2
  84.6 0.0 copy-start.3
  84.6 5.9 %shard_map.98 = f32[16,8,128]{2,1,0:T(8,128)} custom-call(s32[648]{0:T(1024)S(1)} %get-tuple-element.18.src, s32[648]{0:T(1024)S(1)} %get-tuple-element.19.tgt, s32[1]{0:T(128)} %get-tuple-element.20.total, bf16[32,256,128]{2,1,0:T(8,128)(2,1)S(1)} %copy-done.10, bf16[64,16384]{1,0:T(8,128)(2,1)S(1)} %bitcast.14, f32[32,4,128]{2,1,0:T(4,128)S(1)} %all_to_all.26.level, ...), custom_call_target="tpu_custom_call" | custom-call | flops 10000000000 | bytes 20000000 | tf_op jit(solution)/shard_map/pallas_call | solution.py:376
  90.5 8.7 %all-to-all-start.3 = ((f32[16,8,128]{2,1,0:T(8,128)}), f32[16,8,128]{2,1,0:T(8,128)S(1)}, u32[]{:S(2)}, u32[]{:S(2)}) async-start(f32[16,8,128]{2,1,0:T(8,128)} %shard_map.98), calls=%async_computation.3 | async-start | bytes 131072 | tf_op jit(solution)/shard_map/all_to_all | solution.py:56
  99.2 0.0 copy-done.1
  99.2 0.9 shard_map.99.moments
  100.2 6.9 %all-to-all-done.3.arrived = f32[16,8,128]{2,1,0:T(8,128)S(1)} async-done(((f32[16,8,128]{2,1,0:T(8,128)}), f32[16,8,128]{2,1,0:T(8,128)S(1)}, u32[]{:S(2)}, u32[]{:S(2)}) %all-to-all-start.3) | async-done | bytes 65568 | tf_op jit(solution)/shard_map/all_to_all | solution.py:56
  107.1 0.6 shard_map.100
  107.7 4.7 %all-to-all-start.4 = ((f32[32,1,128]{2,1,0:T(1,128)}), f32[32,1,128]{2,1,0:T(1,128)S(1)}, u32[]{:S(2)}, u32[]{:S(2)}) async-start(f32[32,1,128]{2,1,0:T(1,128)} %get-tuple-element.26), calls=%async_computation.4 | async-start | bytes 32768 | tf_op jit(solution)/shard_map/all_to_all | solution.py:56
  112.4 8.6 %all-to-all-done.4.arrived = f32[32,1,128]{2,1,0:T(1,128)S(1)} async-done(((f32[32,1,128]{2,1,0:T(1,128)}), f32[32,1,128]{2,1,0:T(1,128)S(1)}, u32[]{:S(2)}, u32[]{:S(2)}) %all-to-all-start.4) | async-done | bytes 16416 | tf_op jit(solution)/shard_map/all_to_all | solution.py:56
  121.0 0.0 copy-done.2
  121.0 0.0 copy-done.3
  121.0 0.0 copy-start.5
  121.0 0.7 copy-done.5
  121.7 0.9 shard_map.101
  122.5 0.6 copy.13
  (1 shorter events, 0.0 us)
Async XLA Ops:
  7.2 11.0 %copy-start.11 = (s32[32,20]{0,1:T(8,128)S(1)}, s32[32,20]{0,1:T(8,128)}, u32[]{:S(2)}) copy-start(s32[32,20]{0,1:T(8,128)} %param.10) | copy-start | bytes 7684
  7.2 11.1 %copy-start.4 = (f32[8192]{0:T(1024)S(1)}, f32[8192]{0:T(1024)}, u32[]{:S(2)}) copy-start(f32[8192]{0:T(1024)} %param.9) | copy-start | bytes 98308
  8.0 12.1 %copy-start.6 = (s32[32]{0:T(128)S(1)}, s32[32]{0:T(128)}, u32[]{:S(2)}) copy-start(s32[32]{0:T(128)} %counts.1) | copy-start | bytes 388
  9.0 22.4 %all-to-all-start = ((bf16[8,256,128]{2,1,0:T(8,128)(2,1)}), bf16[8,256,128]{2,1,0:T(8,128)(2,1)S(1)}, u32[]{:S(2)}, u32[]{:S(2)}) async-start(bf16[8,256,128]{2,1,0:T(8,128)(2,1)} %broadcast_in_dim.2), calls=%async_computation | async-start | bytes 1048576 | tf_op jit(solution)/shard_map/all_to_all | solution.py:56
  16.6 63.5 %all-gather.3.cloned.1.call-start = ((), (), s32[]{:S(2)}) async-start(), calls=%async_computation.5 | async-start | bytes 1114112 | tf_op jit(solution)/shard_map/all_gather | solution.py:345
  31.4 7.1 %collective-permute-start = (bf16[8,256,128]{2,1,0:T(8,128)(2,1)S(1)}, bf16[8,256,128]{2,1,0:T(8,128)(2,1)S(1)}, u32[]{:S(2)}, u32[]{:S(2)}) collective-permute-start(bf16[8,256,128]{2,1,0:T(8,128)(2,1)S(1)} %all-to-all-done.mine), channel_id=1, source_target_pairs={{0,1},{1,0},{2,3},{3,2},{4,5},{5,4},{6,7},{7,6},{8,9},{9,8},{10,11... | collective-permute-start | bytes 1572872 | tf_op jit(solution)/shard_map/ppermute | solution.py:343
  38.5 1.6 %copy-start.7 = (bf16[16384,64]{0,1:T(8,128)(2,1)S(1)}, bf16[16384,64]{0,1:T(8,128)(2,1)}, u32[]{:S(2)}) copy-start(bf16[16384,64]{0,1:T(8,128)(2,1)} %param.8) | copy-start | bytes 6291460
  45.2 1.3 %copy-start.9 = (bf16[32,256,128]{2,1,0:T(8,128)(2,1)}, bf16[32,256,128]{2,1,0:T(8,128)(2,1)S(1)}, u32[]{:S(2)}) copy-start(bf16[32,256,128]{2,1,0:T(8,128)(2,1)S(1)} %get-tuple-element.23.x) | copy-start | bytes 6291460
  80.2 1.2 copy-start
  81.4 1.6 %copy-start.8 = (bf16[16384,64]{0,1:T(8,128)(2,1)S(1)}, bf16[16384,64]{0,1:T(8,128)(2,1)}, u32[]{:S(2)}) copy-start(bf16[16384,64]{0,1:T(8,128)(2,1)} %param.8) | copy-start | bytes 6291460
  83.0 1.6 %copy-start.10 = (bf16[32,256,128]{2,1,0:T(8,128)(2,1)S(1)}, bf16[32,256,128]{2,1,0:T(8,128)(2,1)}, u32[]{:S(2)}) copy-start(bf16[32,256,128]{2,1,0:T(8,128)(2,1)} %copy-done.9) | copy-start | bytes 6291460
  84.6 14.6 %copy-start.1 = (f32[512,512]{1,0:T(8,128)S(1)}, f32[512,512]{1,0:T(8,128)}, u32[]{:S(2)}) copy-start(f32[512,512]{1,0:T(8,128)} %all-gather.3.cloned.1.call-done) | copy-start | bytes 3145732
  84.6 36.4 %copy-start.2 = (f32[8,512]{1,0:T(8,128)S(1)}, f32[8,512]{1,0:T(8,128)}, u32[]{:S(2)}) copy-start(f32[8,512]{1,0:T(8,128)} %slopes.1) | copy-start | bytes 49156
  84.6 36.4 %copy-start.3 = (f32[8,512]{1,0:T(8,128)S(1)}, f32[8,512]{1,0:T(8,128)}, u32[]{:S(2)}) copy-start(f32[8,512]{1,0:T(8,128)} %steps.1) | copy-start | bytes 49156
  90.5 16.6 %all-to-all-start.3 = ((f32[16,8,128]{2,1,0:T(8,128)}), f32[16,8,128]{2,1,0:T(8,128)S(1)}, u32[]{:S(2)}, u32[]{:S(2)}) async-start(f32[16,8,128]{2,1,0:T(8,128)} %shard_map.98), calls=%async_computation.3 | async-start | bytes 131072 | tf_op jit(solution)/shard_map/all_to_all | solution.py:56
  107.7 13.3 %all-to-all-start.4 = ((f32[32,1,128]{2,1,0:T(1,128)}), f32[32,1,128]{2,1,0:T(1,128)S(1)}, u32[]{:S(2)}, u32[]{:S(2)}) async-start(f32[32,1,128]{2,1,0:T(1,128)} %get-tuple-element.26), calls=%async_computation.4 | async-start | bytes 32768 | tf_op jit(solution)/shard_map/all_to_all | solution.py:56
  121.0 0.7 copy-start.5
Sparse Core Ops, SparseCore 0:
  20.2 46.2 all-gather.2

commit v3 on v2

--- a/solution.py
+++ b/solution.py
@@ -19,11 +19,15 @@
 entropy = 0.5
 SCALE = LOG2E / entropy
 UNROLL = 8
+PLACE = 1 << 16
 WIDE = 64
 F32 = jnp.float32
 
 VMEM = pl.BlockSpec(memory_space=pltpu.VMEM)
 SMEM = pl.BlockSpec(memory_space=pltpu.SMEM)
+
+
+COST = pl.CostEstimate(flops=10**10, bytes_accessed=10**6, transcendentals=0)
 
 
 def call(body, out_shape, ins, outs, scratch=(), cost=None):
@@ -60,15 +64,17 @@
     return swap(jnp.broadcast_to(x[None], (lax.axis_size(axis), *x.shape)), axis)
 
 
-def listing_kernel(blocks, own_blocks, rank, block_map, counts, src, tgt, total):
+def listing_kernel(blocks, own_blocks, rank, block_map, counts, pairs, total):
     first = rank[0] * own_blocks
+    core = rank[1]
 
     def of_block(b, n):
         count = counts[b]
+        far = (lax.rem(lax.shift_right_logical(b, 1), 2) != core).astype(jnp.int32)
+        place = far * (blocks // 2) + 2 * lax.shift_right_logical(b, 2) + lax.rem(b, 2)
         for k in range(block_map.shape[1]):
             local = block_map[b, k] - first
-            src[n] = b
-            tgt[n] = local
+            pairs[n] = place * PLACE + local
             mine = (k < count) & (local >= 0) & (local < own_blocks)
             n = n + mine.astype(jnp.int32)
         return n
@@ -76,8 +82,7 @@
     n = lax.fori_loop(0, blocks, of_block, jnp.int32(0))
     total[0] = n
     for extra in range(UNROLL):
-        src[n + extra] = blocks
-        tgt[n + extra] = own_blocks
+        pairs[n + extra] = blocks * PLACE + own_blocks
 
 
 def split_three(value):
@@ -87,33 +92,39 @@
     return high, middle, rest - middle
 
 
-def columns_kernel(pot, out):
-    row = lax.broadcasted_iota(jnp.int32, (HALF, HALF), 0)
-    ones = jnp.where((row >= WIDE + 3) & (row < WIDE + 6), 1.0, 0.0)
-
-    def turn(c, carry):
-        parts = split_three(pot[pl.ds(c, 1), :])
-        tile = ones
-        for k in range(3):
-            tile = jnp.where(row == WIDE + k, parts[k], tile)
-        at = pl.ds(pl.multiple_of(lax.rem(c, 2) * HALF, HALF), HALF)
-        out[lax.shift_right_logical(c, 1), at, :] = jnp.transpose(tile).astype(jnp.bfloat16)
-        return carry
-
-    lax.fori_loop(0, pot.shape[0], turn, 0, unroll=4)
-
-
-def lay_out(rank, mine, other, columns, x):
+def columns_kernel(rank, pot, out, tile):
     core = rank[1]
+    tile[...] = jnp.zeros(tile.shape, F32)
+    ys = pot.shape[0] // 8
+    for h in range(2):
+        for far in range(2):
+            for y in range(ys):
+                for half in range(2):
+                    side = 1 - core if far else core
+                    parts = split_three(pot[pl.ds(8 * y + 4 * side + 2 * half + h, 1), :])
+                    for k in range(3):
+                        at = 4 * (2 * ys * far + 2 * y + half) + k
+                        tile[at : at + 1, :] = parts[k]
+        out[h * HALF : (h + 1) * HALF, :] = jnp.transpose(tile[...]).astype(jnp.bfloat16)
+
+
+def turned(value, by):
+    return jnp.concatenate([value[:, by:], value[:, :by]], axis=1) if by % HALF else value
+
+
+def lay_out(mine, other, columns, x):
     lane = lax.broadcasted_iota(jnp.int32, (BLOCK, HALF), 1)
-    for arrived, side in ((mine, core), (other, 1 - core)):
+    ones = jnp.where((lane >= WIDE + 3) & (lane < WIDE + 6), 1.0, 0.0).astype(jnp.bfloat16)
+    own = columns[...]
+    place = 0
+    for arrived in (mine, other):
         for y in range(arrived.shape[0]):
             piece = arrived[y]
             for half in range(2):
-                b = 4 * y + 2 * side + half
-                if half:
-                    piece = jnp.concatenate([piece[:, WIDE:], piece[:, :WIDE]], axis=1)
-                x[b] = jnp.where(lane < WIDE, piece, columns[b])
+                parts = turned(own, (4 * place - WIDE) % HALF)
+                rest = jnp.where((lane >= WIDE) & (lane < WIDE + 3), parts, ones)
+                x[place] = jnp.where(lane < WIDE, turned(piece, WIDE * half), rest)
+                place += 1
 
 
 def target_columns(t, tb, h, extra):
@@ -123,9 +134,9 @@
 
 
 def column_kernel(
-    blocks, own_blocks, rank, src, tgt, total, mine, other, t, columns, out, x, peak, acc
+    blocks, own_blocks, listed, total, mine, other, t, columns, out, x, peak, acc
 ):
-    lay_out(rank, mine, other, columns, x)
+    lay_out(mine, other, columns, x)
     peak[...] = jnp.full(peak.shape, NEG, F32)
     acc[...] = jnp.zeros(acc.shape, F32)
     live = total[0]
@@ -135,8 +146,9 @@
     def turn(step, carry):
         found = []
         for u in range(UNROLL):
-            b_all = src[step * UNROLL + u]
-            t_all = tgt[step * UNROLL + u]
+            pair = listed[step * UNROLL + u]
+            b_all = lax.shift_right_logical(pair, 16)
+            t_all = lax.bitwise_and(pair, PLACE - 1)
             b = jnp.minimum(b_all, blocks - 1)
             tb = jnp.minimum(t_all, own_blocks - 1)
             rows = x[b]
@@ -179,16 +191,16 @@
     whole = jnp.zeros_like(top)
     for p in range(peers):
         whole = whole + jnp.exp2(arrived[p] - top)
-    level = (-entropy * LN2) * (top + jnp.log2(whole))
+    level = top + jnp.log2(whole)
     for p in range(peers):
         out[p] = level
 
 
-def moments_kernel(peers, stored, pairs, out, square):
+def moments_kernel(stored, near, far, out, square):
     total = jnp.zeros((2 * stored, 2 * stored), F32)
-    for p in range(peers):
-        rows = pairs[p, : 2 * stored, :]
-        total = total + nt(rows, rows, lax.Precision.HIGHEST)
+    for pairs in (near, far):
+        for p in range(pairs.shape[0]):
+            total = total + nt(pairs[p], pairs[p], lax.Precision.HIGHEST)
     square[...] = jnp.zeros(square.shape, F32)
     square[:, : 2 * stored] = total
     lane = lax.broadcasted_iota(jnp.int32, (1, HALF), 1)
@@ -202,8 +214,26 @@
 
 
 def row_kernel(
-    blocks, own_blocks, ratio, peers, src, tgt, total, x, t, level, pairs, out, acc, sums
+    blocks,
+    own_blocks,
+    ratio,
+    peers,
+    rank,
+    listed,
+    total,
+    mine,
+    other,
+    t,
+    columns,
+    level,
+    near,
+    far,
+    out,
+    x,
+    acc,
+    sums,
 ):
+    lay_out(mine, other, columns, x)
     acc[...] = jnp.zeros(acc.shape, F32)
     live = total[0]
     row = lax.broadcasted_iota(jnp.int32, (16, HALF), 0)
@@ -212,8 +242,9 @@
     def turn(step, carry):
         found = []
         for u in range(UNROLL):
-            b_all = src[step * UNROLL + u]
-            t_all = tgt[step * UNROLL + u]
+            pair = listed[step * UNROLL + u]
+            b_all = lax.shift_right_logical(pair, 16)
+            t_all = lax.bitwise_and(pair, PLACE - 1)
             b = jnp.minimum(b_all, blocks - 1)
             tb = jnp.minimum(t_all, own_blocks - 1)
             rows = x[b]
@@ -223,7 +254,7 @@
                     lax.shift_right_logical(tb, 1), pl.ds(lax.rem(tb, 2) * 2 + h, 1), :
                 ]
                 extra = ones
-                for k, part in enumerate(split_three(line)):
+                for k, part in enumerate(split_three((-entropy * LN2) * line)):
                     extra = jnp.where(row == 3 + k, part, extra)
                 e = jnp.exp2(nn(rows, target_columns(t, tb, h, extra)) * SCALE)
                 parts = e if parts is None else parts + e
@@ -243,27 +274,32 @@
 
     lax.fori_loop(0, blocks, fold, 0, unroll=4)
 
-    rows_kept = pairs.shape[1] // 2
+    rows_kept = near.shape[1]
     lane = lax.broadcasted_iota(jnp.int32, (rows_kept, HALF), 1)
     row = lax.broadcasted_iota(jnp.int32, (rows_kept, HALF), 0)
     dots = jnp.zeros((rows_kept, HALF), F32)
-    for p in range(blocks // 2):
-        part = 1.0 / peers - ratio * sums[p]
-        out[p, :4, :] = part
-        for q in range(4):
-            at = slice(q * HALF, (q + 1) * HALF)
-            dots = dots + pairs[p, :rows_kept, at] * part[q : q + 1]
+    core = rank[1]
+    place = 0
+    for pairs, side in ((near, core), (far, 1 - core)):
+        for y in range(pairs.shape[0]):
+            part = 1.0 / peers - ratio * sums[place]
+            place += 1
+            out[2 * y + side, :4, :] = part
+            for q in range(4):
+                at = slice(q * HALF, (q + 1) * HALF)
+                dots = dots + pairs[y, :, at] * part[q : q + 1]
     spread = jnp.where(lane == row, jnp.sum(dots, axis=1, keepdims=True), 0.0)
     value = jnp.sum(spread, axis=0, keepdims=True)
     for p in range(blocks // 2):
         out[p, 4:5, :] = value
 
 
-def gradient_kernel(peers, src_size, arrived, moments, gradient, dots):
+def gradient_kernel(peers, src_size, arrived, moments, gradient, again, dots):
     whole = arrived[0]
     for p in range(1, peers):
         whole = whole + arrived[p]
     gradient[...] = whole[:4]
+    again[...] = whole[:4]
     value = whole[4:5] + moments[...]
     for p in range(src_size):
         dots[p] = value
@@ -326,34 +362,41 @@
     mine = share(packed, TGT[0])
     core = lax.axis_index(TGT[1])
     t = targets.T
+    rank = jnp.stack([lax.axis_index(TGT), core]).astype(jnp.int32)
     columns = call(
-        columns_kernel, sds((blocks, BLOCK, HALF), jnp.bfloat16), [VMEM], VMEM
-    )(potential.reshape(-1, HALF))
-
-    rank = jnp.stack([lax.axis_index(TGT), core]).astype(jnp.int32)
+        columns_kernel,
+        sds((BLOCK, HALF), jnp.bfloat16),
+        [SMEM, VMEM],
+        VMEM,
+        [pltpu.VMEM((HALF, HALF), F32)],
+    )(rank, potential.reshape(-1, HALF))
     slots = blocks * listed + UNROLL
-    src, tgt, total = call(
+    pairs, total = call(
         functools.partial(listing_kernel, blocks, own_blocks),
-        (sds((slots,), jnp.int32), sds((slots,), jnp.int32), sds((1,), jnp.int32)),
+        (sds((slots,), jnp.int32), sds((1,), jnp.int32)),
         [SMEM] * 3,
-        [SMEM] * 3,
+        [SMEM] * 2,
     )(rank, block_map, counts)
 
-    mine, columns, src, tgt, total = lax.optimization_barrier((mine, columns, src, tgt, total))
+    mine, columns, pairs, total = lax.optimization_barrier((mine, columns, pairs, total))
     other = lax.ppermute(mine, TGT[1], [(0, 1), (1, 0)])
-    history = jnp.concatenate([step_history, slope_history] * 2, axis=0)
-    pairs = lax.all_gather(history, TGT)
-
-    levels, x = call(
+    history = jnp.concatenate([step_history, slope_history], axis=0)
+    mine, history = lax.optimization_barrier((mine, history))
+    near = share(history, TGT[0])
+
+    rows = pltpu.VMEM((blocks, BLOCK, HALF), jnp.bfloat16)
+    levels = call(
         functools.partial(column_kernel, blocks, own_blocks),
-        (sds((src_size, 4, HALF)), sds((blocks, BLOCK, HALF), jnp.bfloat16)),
-        [SMEM] * 4 + [VMEM] * 4,
-        [VMEM] * 2,
-        [pltpu.VMEM((8 * own_blocks + 8, BLOCK), F32)] * 2,
-        pl.CostEstimate(flops=10**10, bytes_accessed=2 * 10**7, transcendentals=4 * 10**6),
-    )(rank, src, tgt, total, mine, other, t, columns)
-
+        sds((src_size, 4, HALF)),
+        [SMEM] * 2 + [VMEM] * 4,
+        VMEM,
+        [rows] + [pltpu.VMEM((8 * own_blocks + 8, BLOCK), F32)] * 2,
+        COST,
+    )(pairs, total, mine, other, t, columns)
+
+    levels, near = lax.optimization_barrier((levels, near))
     arrived = swap(levels, SRC)
+    far = lax.ppermute(near, TGT[1], [(0, 1), (1, 0)])
 
     level = call(
         functools.partial(combine_kernel, src_size),
@@ -362,35 +405,39 @@
         VMEM,
     )(arrived)
     level = swap(level, SRC)
-    target_potential = level.reshape(-1)
+    target_potential = (-entropy * LN2) * level.reshape(-1)
 
     moments = call(
-        functools.partial(moments_kernel, tgt_size, stored),
+        functools.partial(moments_kernel, stored),
         sds((1, HALF)),
-        [VMEM],
+        [VMEM] * 2,
         VMEM,
         [pltpu.VMEM((2 * stored, HALF), F32)],
-    )(pairs)
+    )(near, far)
 
     ratio = blocks * src_size / (own_blocks * tgt_size)
     parts = call(
         functools.partial(row_kernel, blocks, own_blocks, ratio, tgt_size),
         sds((tgt_size, 8, HALF)),
-        [SMEM] * 3 + [VMEM] * 4,
+        [SMEM] * 3 + [VMEM] * 7,
         VMEM,
-        [pltpu.VMEM((blocks + 1, BLOCK, HALF), F32), pltpu.VMEM((tgt_size, 4, HALF), F32)],
-        pl.CostEstimate(flops=10**10, bytes_accessed=2 * 10**7, transcendentals=4 * 10**6),
-    )(src, tgt, total, x, t, level, pairs)
-
-    gradient, dots = call(
+        [
+            rows,
+            pltpu.VMEM((blocks + 1, BLOCK, HALF), F32),
+            pltpu.VMEM((tgt_size, 4, HALF), F32),
+        ],
+        COST,
+    )(rank, pairs, total, mine, other, t, columns, level, near, far)
+
+    gradient, again, dots = call(
         functools.partial(gradient_kernel, tgt_size, src_size),
-        (sds((4, HALF)), sds((src_size, 1, HALF))),
+        (sds((4, HALF)), sds((4, HALF)), sds((src_size, 1, HALF))),
         [VMEM] * 2,
-        [VMEM] * 2,
+        [VMEM] * 3,
     )(swap(parts, TGT), moments)
     direction = call(
         functools.partial(direction_kernel, src_size, stored), sds((4, HALF)), [VMEM] * 4, VMEM
-    )(swap(dots, SRC), gradient, step_history, slope_history)
+    )(swap(dots, SRC), again, step_history, slope_history)
     return (gradient.reshape(-1), direction.reshape(-1), target_potential)
 
 

time: 131 us -> 120 us (0.916)
  between operations: 14.2 us -> 0.79 us
  local copies, waits for them, and re-layouts: 10.6 us -> 3.44 us
  waiting for transfers between devices: 24 us -> 30.2 us
  starting transfers between devices: 26.7 us -> 30.4 us
    unnamed x26 -> x11, local copies, waits for them, and re-layouts: 8.79 us -> 0.8 us
    all_to_all x3 -> x4, waiting for transfers between devices: 22.4 us -> 30.2 us  [swap(): return lax.all_to_all(x, axis, 0, 0, tiled=True)]
    ppermute x0 -> x1, starting transfers between devices: none -> 2.34 us  [per_device(): far = lax.ppermute(near, TGT[1], [(0, 1), (1, 0)])]
    ppermute x1, waiting for transfers between devices: 1.51 us -> 0.01 us  [per_device(): other = lax.ppermute(mine, TGT[1], [(0, 1), (1, 0)])]
    concatenate x1, other arithmetic: 1.43 us -> 0.01 us  [per_device(): history = jnp.concatenate([step_history, slope_history], axis=0)]
    all_to_all x3 -> x4, starting transfers between devices: 21.1 us -> 22.5 us  [swap(): return lax.all_to_all(x, axis, 0, 0, tiled=True)]
  transfers between devices with their start and end apart: 5 -> 6, of which waited for: 4 -> 4; matrix products, arithmetic and copies ran while one was open for 1% -> 2% of each run, Pallas kernels for 9% -> 10%
where the time goes in v3:
time: 120 us
  blocking collectives  33.6 us (28%)
  starting transfers between devices  30.4 us (25%)
  waiting for transfers between devices  30.2 us (25%)
  Pallas kernels  20.4 us (17%)
  local copies, waits for them, and re-layouts  3.44 us (3%)
    all_to_all x2, blocking collectives, swap(): return lax.all_to_all(x, axis, 0, 0, tiled=True)  33.6 us
    all_to_all x4, waiting for transfers between devices, swap(): return lax.all_to_all(x, axis, 0, 0, tiled=True)  30.2 us
    all_to_all x4, starting transfers between devices, swap(): return lax.all_to_all(x, axis, 0, 0, tiled=True)  22.5 us
    pallas_call x1, Pallas kernels, per_device(): call(functools.partial(row_kernel, blocks, own_blocks, ratio, tgt_size),...  7.07 us
    pallas_call x1, Pallas kernels, per_device(): call(functools.partial(column_kernel, blocks, own_blocks), sds((src_size,...  5.88 us
    ppermute x1, starting transfers between devices, per_device(): other = lax.ppermute(mine, TGT[1], [(0, 1), (1, 0)])  5.6 us
    pallas_call x1, Pallas kernels, per_device(): call(functools.partial(listing_kernel, blocks, own_blocks), (sds((slots,)...  4.25 us
  transfers between devices with their start and end apart: 6, of which 4 were waited for; matrix products, arithmetic and copies ran while one was open for 2% of the time, Pallas kernels for 10%

profile of v3, /device:TPU:1, one launch (start us, length us, event | category | flops | bytes accessed | tf_op | source)
XLA Modules:
  0.0 119.6 jit_solution(14792424596959091023)
XLA Ops:
  0.6 0.0 copy-start.2
  0.6 0.0 copy-start.3
  0.7 0.0 copy-start
  0.7 0.0 copy-start.1
  0.7 0.0 copy-start.4
  0.7 0.9 fusion
  1.6 0.1 copy.10
  1.7 0.9 broadcast_in_dim.4
  2.6 7.7 %all-to-all-start = ((bf16[8,256,128]{2,1,0:T(8,128)(2,1)}), bf16[8,256,128]{2,1,0:T(8,128)(2,1)S(1)}, u32[]{:S(2)}, u32[]{:S(2)}) async-start(bf16[8,256,128]{2,1,0:T(8,128)(2,1)} %broadcast_in_dim.4), calls=%async_computation | async-start | bytes 1048576 | tf_op jit(solution)/shard_map/all_to_all | solution.py:60
  10.3 0.8 copy.11.block_map
  11.0 0.1 pad_add_fusion.rank
  11.1 0.0 copy-done.2
  11.1 0.7 shard_map.94.columns
  11.8 0.0 copy-done.3
  11.8 4.3 %shard_map.95 = (s32[648]{0:T(1024)S(1)}, s32[1]{0:T(128)}) custom-call(s32[2]{0:T(128)S(1)} %pad_add_fusion.rank, s32[32,20]{1,0:T(8,128)S(1)} %copy.11.block_map, s32[32]{0:T(128)S(1)} %copy-done.3), custom_call_target="tpu_custom_call" | custom-call | tf_op jit(solution)/shard_map/pallas_call | solution.py:374
  16.1 8.9 %all-to-all-done.mine = bf16[8,256,128]{2,1,0:T(8,128)(2,1)S(1)} async-done(((bf16[8,256,128]{2,1,0:T(8,128)(2,1)}), bf16[8,256,128]{2,1,0:T(8,128)(2,1)S(1)}, u32[]{:S(2)}, u32[]{:S(2)}) %all-to-all-start) | async-done | bytes 524320 | tf_op jit(solution)/shard_map/all_to_all | solution.py:60
  25.0 5.6 %collective-permute-start = (bf16[8,256,128]{2,1,0:T(8,128)(2,1)S(1)}, bf16[8,256,128]{2,1,0:T(8,128)(2,1)}, u32[]{:S(2)}, u32[]{:S(2)}) collective-permute-start(bf16[8,256,128]{2,1,0:T(8,128)(2,1)S(1)} %all-to-all-done.mine), channel_id=1, source_target_pairs={{0,1},{1,0},{2,3},{3,2},{4,5},{5,4},{6,7},{7,6},{8,9},{9,8},{10,11... | collective-permute-start | bytes 1572872 | tf_op jit(solution)/shard_map/ppermute | solution.py:382
  30.6 0.0 copy-done
  30.6 0.0 copy-done.1
  30.6 0.7 broadcast_in_dim.5
  31.4 3.4 %all-to-all-start.1 = ((f32[8,16,512]{2,1,0:T(8,128)}), f32[8,16,512]{2,1,0:T(8,128)S(1)}, u32[]{:S(2)}, u32[]{:S(2)}) async-start(f32[8,16,512]{2,1,0:T(8,128)} %broadcast_in_dim.5), calls=%async_computation.1 | async-start | bytes 524288 | tf_op jit(solution)/shard_map/all_to_all | solution.py:60
  34.8 0.0 collective-permute-done.other
  34.8 0.0 copy-done.4
  34.8 5.9 %shard_map.96 = f32[32,4,128]{2,1,0:T(4,128)S(1)} custom-call(s32[648]{0:T(1024)S(1)} %get-tuple-element.18.listed, s32[1]{0:T(128)} %get-tuple-element.19.total, bf16[8,256,128]{2,1,0:T(8,128)(2,1)S(1)} %all-to-all-done.mine, bf16[8,256,128]{2,1,0:T(8,128)(2,1)} %collective-permute-done.other, bf16[64,16384]{1,0:T(8,128)(2,1)S(1)} %bitcast.8, ...), custom_call_target="tpu_custom_call" | custom-call | flops 10000000000 | bytes 1000000 | tf_op jit(solution)/shard_map/pallas_call | solution.py:388
  40.7 6.4 %all-to-all-done.1.near = f32[8,16,512]{2,1,0:T(8,128)S(1)} async-done(((f32[8,16,512]{2,1,0:T(8,128)}), f32[8,16,512]{2,1,0:T(8,128)S(1)}, u32[]{:S(2)}, u32[]{:S(2)}) %all-to-all-start.1) | async-done | bytes 262176 | tf_op jit(solution)/shard_map/all_to_all | solution.py:60
  47.1 2.3 %collective-permute-start.1 = (f32[8,16,512]{2,1,0:T(8,128)S(1)}, f32[8,16,512]{2,1,0:T(8,128)S(1)}, u32[]{:S(2)}, u32[]{:S(2)}) collective-permute-start(f32[8,16,512]{2,1,0:T(8,128)S(1)} %all-to-all-done.1.near), channel_id=1, source_target_pairs={{0,1},{1,0},{2,3},{3,2},{4,5},{5,4},{6,7},{7,6},{8,9},{9,8},{10,11... | collective-permute-start | bytes 786440 | tf_op jit(solution)/shard_map/ppermute | solution.py:399
  49.4 21.6 %all_to_all.30.arrived = f32[32,4,128]{2,1,0:T(4,128)S(1)} all-to-all(f32[32,4,128]{2,1,0:T(4,128)S(1)} %shard_map.96), channel_id=1, replica_groups=mesh['src_0'=4,'src_1'=8,'tgt_0'=8,'tgt_1'=2] {'src_0','src_1'}, dimensions={0} | all-to-all | bytes 131072 | tf_op jit(solution)/shard_map/all_to_all | solution.py:60
  71.0 0.1 shard_map.97
  71.1 12.1 %all_to_all.31.level = f32[32,4,128]{2,1,0:T(4,128)S(1)} all-to-all(f32[32,4,128]{2,1,0:T(4,128)S(1)} %shard_map.97), channel_id=1, replica_groups=mesh['src_0'=4,'src_1'=8,'tgt_0'=8,'tgt_1'=2] {'src_0','src_1'}, dimensions={0} | all-to-all | bytes 131072 | tf_op jit(solution)/shard_map/all_to_all | solution.py:60
  83.2 0.0 collective-permute-done.1.far
  83.2 7.1 %shard_map.98 = f32[16,8,128]{2,1,0:T(8,128)} custom-call(s32[2]{0:T(128)S(1)} %pad_add_fusion.rank, s32[648]{0:T(1024)S(1)} %get-tuple-element.18.listed, s32[1]{0:T(128)} %get-tuple-element.19.total, bf16[8,256,128]{2,1,0:T(8,128)(2,1)S(1)} %all-to-all-done.mine, bf16[8,256,128]{2,1,0:T(8,128)(2,1)} %collective-permute-done.other, ...), custom_call_target="tpu_custom_call" | custom-call | flops 10000000000 | bytes 1000000 | tf_op jit(solution)/shard_map/pallas_call | solution.py:419
  90.2 7.7 %all-to-all-start.4 = ((f32[16,8,128]{2,1,0:T(8,128)}), f32[16,8,128]{2,1,0:T(8,128)S(1)}, u32[]{:S(2)}, u32[]{:S(2)}) async-start(f32[16,8,128]{2,1,0:T(8,128)} %shard_map.98), calls=%async_computation.4 | async-start | bytes 131072 | tf_op jit(solution)/shard_map/all_to_all | solution.py:60
  97.9 0.9 shard_map.99.moments
  98.8 6.9 %all-to-all-done.4.arrived = f32[16,8,128]{2,1,0:T(8,128)S(1)} async-done(((f32[16,8,128]{2,1,0:T(8,128)}), f32[16,8,128]{2,1,0:T(8,128)S(1)}, u32[]{:S(2)}, u32[]{:S(2)}) %all-to-all-start.4) | async-done | bytes 65568 | tf_op jit(solution)/shard_map/all_to_all | solution.py:60
  105.7 0.6 shard_map.100
  106.4 3.7 %all-to-all-start.5 = ((f32[32,1,128]{2,1,0:T(1,128)}), f32[32,1,128]{2,1,0:T(1,128)S(1)}, u32[]{:S(2)}, u32[]{:S(2)}) async-start(f32[32,1,128]{2,1,0:T(1,128)} %get-tuple-element.27), calls=%async_computation.5 | async-start | bytes 32768 | tf_op jit(solution)/shard_map/all_to_all | solution.py:60
  110.1 0.6 broadcast_multiply_fusion
  110.8 8.0 %all-to-all-done.5.arrived = f32[32,1,128]{2,1,0:T(1,128)S(1)} async-done(((f32[32,1,128]{2,1,0:T(1,128)}), f32[32,1,128]{2,1,0:T(1,128)S(1)}, u32[]{:S(2)}, u32[]{:S(2)}) %all-to-all-start.5) | async-done | bytes 16416 | tf_op jit(solution)/shard_map/all_to_all | solution.py:60
  118.8 0.9 shard_map.101
  (2 shorter events, 0.0 us)
Async XLA Ops:
  0.6 10.5 %copy-start.2 = (f32[8192]{0:T(1024)S(1)}, f32[8192]{0:T(1024)}, u32[]{:S(2)}) copy-start(f32[8192]{0:T(1024)} %param.9) | copy-start | bytes 98308
  0.6 11.2 %copy-start.3 = (s32[32]{0:T(128)S(1)}, s32[32]{0:T(128)}, u32[]{:S(2)}) copy-start(s32[32]{0:T(128)} %counts.1) | copy-start | bytes 388
  0.7 30.0 %copy-start = (f32[8,512]{1,0:T(8,128)S(1)}, f32[8,512]{1,0:T(8,128)}, u32[]{:S(2)}) copy-start(f32[8,512]{1,0:T(8,128)} %slopes.1) | copy-start | bytes 49156
  0.7 30.0 %copy-start.1 = (f32[8,512]{1,0:T(8,128)S(1)}, f32[8,512]{1,0:T(8,128)}, u32[]{:S(2)}) copy-start(f32[8,512]{1,0:T(8,128)} %steps.1) | copy-start | bytes 49156
  0.7 34.1 %copy-start.4 = (bf16[16384,64]{0,1:T(8,128)(2,1)S(1)}, bf16[16384,64]{0,1:T(8,128)(2,1)}, u32[]{:S(2)}) copy-start(bf16[16384,64]{0,1:T(8,128)(2,1)} %param.8) | copy-start | bytes 6291460
  2.6 22.4 %all-to-all-start = ((bf16[8,256,128]{2,1,0:T(8,128)(2,1)}), bf16[8,256,128]{2,1,0:T(8,128)(2,1)S(1)}, u32[]{:S(2)}, u32[]{:S(2)}) async-start(bf16[8,256,128]{2,1,0:T(8,128)(2,1)} %broadcast_in_dim.4), calls=%async_computation | async-start | bytes 1048576 | tf_op jit(solution)/shard_map/all_to_all | solution.py:60
  25.0 9.8 %collective-permute-start = (bf16[8,256,128]{2,1,0:T(8,128)(2,1)S(1)}, bf16[8,256,128]{2,1,0:T(8,128)(2,1)}, u32[]{:S(2)}, u32[]{:S(2)}) collective-permute-start(bf16[8,256,128]{2,1,0:T(8,128)(2,1)S(1)} %all-to-all-done.mine), channel_id=1, source_target_pairs={{0,1},{1,0},{2,3},{3,2},{4,5},{5,4},{6,7},{7,6},{8,9},{9,8},{10,11... | collective-permute-start | bytes 1572872 | tf_op jit(solution)/shard_map/ppermute | solution.py:382
  31.4 15.7 %all-to-all-start.1 = ((f32[8,16,512]{2,1,0:T(8,128)}), f32[8,16,512]{2,1,0:T(8,128)S(1)}, u32[]{:S(2)}, u32[]{:S(2)}) async-start(f32[8,16,512]{2,1,0:T(8,128)} %broadcast_in_dim.5), calls=%async_computation.1 | async-start | bytes 524288 | tf_op jit(solution)/shard_map/all_to_all | solution.py:60
  47.1 36.1 %collective-permute-start.1 = (f32[8,16,512]{2,1,0:T(8,128)S(1)}, f32[8,16,512]{2,1,0:T(8,128)S(1)}, u32[]{:S(2)}, u32[]{:S(2)}) collective-permute-start(f32[8,16,512]{2,1,0:T(8,128)S(1)} %all-to-all-done.1.near), channel_id=1, source_target_pairs={{0,1},{1,0},{2,3},{3,2},{4,5},{5,4},{6,7},{7,6},{8,9},{9,8},{10,11... | collective-permute-start | bytes 786440 | tf_op jit(solution)/shard_map/ppermute | solution.py:399
  90.2 15.5 %all-to-all-start.4 = ((f32[16,8,128]{2,1,0:T(8,128)}), f32[16,8,128]{2,1,0:T(8,128)S(1)}, u32[]{:S(2)}, u32[]{:S(2)}) async-start(f32[16,8,128]{2,1,0:T(8,128)} %shard_map.98), calls=%async_computation.4 | async-start | bytes 131072 | tf_op jit(solution)/shard_map/all_to_all | solution.py:60
  106.4 12.4 %all-to-all-start.5 = ((f32[32,1,128]{2,1,0:T(1,128)}), f32[32,1,128]{2,1,0:T(1,128)S(1)}, u32[]{:S(2)}, u32[]{:S(2)}) async-start(f32[32,1,128]{2,1,0:T(1,128)} %get-tuple-element.27), calls=%async_computation.5 | async-start | bytes 32768 | tf_op jit(solution)/shard_map/all_to_all | solution.py:60

commit v4 on v3

--- a/solution.py
+++ b/solution.py
@@ -196,11 +196,8 @@
         out[p] = level
 
 
-def moments_kernel(stored, near, far, out, square):
-    total = jnp.zeros((2 * stored, 2 * stored), F32)
-    for pairs in (near, far):
-        for p in range(pairs.shape[0]):
-            total = total + nt(pairs[p], pairs[p], lax.Precision.HIGHEST)
+def moments_kernel(stored, history, out, square):
+    total = nt(history[...], history[...], lax.Precision.HIGHEST)
     square[...] = jnp.zeros(square.shape, F32)
     square[:, : 2 * stored] = total
     lane = lax.broadcasted_iota(jnp.int32, (1, HALF), 1)
@@ -216,8 +213,6 @@
 def row_kernel(
     blocks,
     own_blocks,
-    ratio,
-    peers,
     rank,
     listed,
     total,
@@ -226,8 +221,6 @@
     t,
     columns,
     level,
-    near,
-    far,
     out,
     x,
     acc,
@@ -274,35 +267,39 @@
 
     lax.fori_loop(0, blocks, fold, 0, unroll=4)
 
-    rows_kept = near.shape[1]
-    lane = lax.broadcasted_iota(jnp.int32, (rows_kept, HALF), 1)
-    row = lax.broadcasted_iota(jnp.int32, (rows_kept, HALF), 0)
-    dots = jnp.zeros((rows_kept, HALF), F32)
     core = rank[1]
     place = 0
-    for pairs, side in ((near, core), (far, 1 - core)):
-        for y in range(pairs.shape[0]):
-            part = 1.0 / peers - ratio * sums[place]
+    for side in (core, 1 - core):
+        for y in range(mine.shape[0]):
+            out[2 * y + side] = sums[place]
             place += 1
-            out[2 * y + side, :4, :] = part
-            for q in range(4):
-                at = slice(q * HALF, (q + 1) * HALF)
-                dots = dots + pairs[y, :, at] * part[q : q + 1]
-    spread = jnp.where(lane == row, jnp.sum(dots, axis=1, keepdims=True), 0.0)
-    value = jnp.sum(spread, axis=0, keepdims=True)
-    for p in range(blocks // 2):
-        out[p, 4:5, :] = value
-
-
-def gradient_kernel(peers, src_size, arrived, moments, gradient, again, dots):
+
+
+def gradient_kernel(peers, ratio, arrived, history, moments, gradient, again, dots):
     whole = arrived[0]
     for p in range(1, peers):
         whole = whole + arrived[p]
-    gradient[...] = whole[:4]
-    again[...] = whole[:4]
-    value = whole[4:5] + moments[...]
-    for p in range(src_size):
+    grad = 1.0 - ratio * whole
+    gradient[...] = grad
+    again[...] = grad
+    rows_kept = history.shape[0]
+    lane = lax.broadcasted_iota(jnp.int32, (rows_kept, HALF), 1)
+    row = lax.broadcasted_iota(jnp.int32, (rows_kept, HALF), 0)
+    total = jnp.zeros((rows_kept, HALF), F32)
+    for q in range(4):
+        total = total + history[:, q * HALF : (q + 1) * HALF] * grad[q : q + 1]
+    spread = jnp.where(lane == row, jnp.sum(total, axis=1, keepdims=True), 0.0)
+    value = jnp.sum(spread, axis=0, keepdims=True) + moments[...]
+    for p in range(peers):
         dots[p] = value
+
+
+def pass_on_kernel(arrived, out):
+    value = arrived[0]
+    for p in range(1, arrived.shape[0]):
+        value = value + arrived[p]
+    for p in range(out.shape[0]):
+        out[p] = value
 
 
 def cross_lane(k, m):
@@ -381,8 +378,13 @@
     mine, columns, pairs, total = lax.optimization_barrier((mine, columns, pairs, total))
     other = lax.ppermute(mine, TGT[1], [(0, 1), (1, 0)])
     history = jnp.concatenate([step_history, slope_history], axis=0)
-    mine, history = lax.optimization_barrier((mine, history))
-    near = share(history, TGT[0])
+    moments = call(
+        functools.partial(moments_kernel, stored),
+        sds((1, HALF)),
+        [VMEM],
+        VMEM,
+        [pltpu.VMEM((2 * stored, HALF), F32)],
+    )(history)
 
     rows = pltpu.VMEM((blocks, BLOCK, HALF), jnp.bfloat16)
     levels = call(
@@ -394,9 +396,7 @@
         COST,
     )(pairs, total, mine, other, t, columns)
 
-    levels, near = lax.optimization_barrier((levels, near))
     arrived = swap(levels, SRC)
-    far = lax.ppermute(near, TGT[1], [(0, 1), (1, 0)])
 
     level = call(
         functools.partial(combine_kernel, src_size),
@@ -407,19 +407,10 @@
     level = swap(level, SRC)
     target_potential = (-entropy * LN2) * level.reshape(-1)
 
-    moments = call(
-        functools.partial(moments_kernel, stored),
-        sds((1, HALF)),
-        [VMEM] * 2,
-        VMEM,
-        [pltpu.VMEM((2 * stored, HALF), F32)],
-    )(near, far)
-
-    ratio = blocks * src_size / (own_blocks * tgt_size)
     parts = call(
-        functools.partial(row_kernel, blocks, own_blocks, ratio, tgt_size),
-        sds((tgt_size, 8, HALF)),
-        [SMEM] * 3 + [VMEM] * 7,
+        functools.partial(row_kernel, blocks, own_blocks),
+        sds((tgt_size, 4, HALF)),
+        [SMEM] * 3 + [VMEM] * 5,
         VMEM,
         [
             rows,
@@ -427,14 +418,16 @@
             pltpu.VMEM((tgt_size, 4, HALF), F32),
         ],
         COST,
-    )(rank, pairs, total, mine, other, t, columns, level, near, far)
-
+    )(rank, pairs, total, mine, other, t, columns, level)
+
+    ratio = blocks * src_size / (own_blocks * tgt_size)
     gradient, again, dots = call(
-        functools.partial(gradient_kernel, tgt_size, src_size),
-        (sds((4, HALF)), sds((4, HALF)), sds((src_size, 1, HALF))),
-        [VMEM] * 2,
+        functools.partial(gradient_kernel, tgt_size, ratio),
+        (sds((4, HALF)), sds((4, HALF)), sds((tgt_size, 1, HALF))),
         [VMEM] * 3,
-    )(swap(parts, TGT), moments)
+        [VMEM] * 3,
+    )(swap(parts, TGT), history, moments)
+    dots = call(pass_on_kernel, sds((src_size, 1, HALF)), [VMEM], VMEM)(swap(dots, TGT))
     direction = call(
         functools.partial(direction_kernel, src_size, stored), sds((4, HALF)), [VMEM] * 4, VMEM
     )(swap(dots, SRC), again, step_history, slope_history)

time: 120 us -> 120 us (level)
  waiting for transfers between devices: 30.2 us -> 34.5 us
  blocking collectives: 33.6 us -> 31.4 us
  starting transfers between devices: 30.4 us -> 28.4 us
    all_to_all x4, waiting for transfers between devices: 30.2 us -> 32.9 us  [swap(): return lax.all_to_all(x, axis, 0, 0, tiled=True)]
    ppermute x1 -> x0, starting transfers between devices: 2.34 us -> none  [per_device(): far = lax.ppermute(near, TGT[1], [(0, 1), (1, 0)])]
    all_to_all x2, blocking collectives: 33.6 us -> 31.4 us  [swap(): return lax.all_to_all(x, axis, 0, 0, tiled=True)]
    ppermute x1, waiting for transfers between devices: 0.01 us -> 1.51 us  [per_device(): other = lax.ppermute(mine, TGT[1], [(0, 1), (1, 0)])]
    pallas_call x3 -> x4, Pallas kernels: 8.62 us -> 8.32 us  [the longest x1 6.86 us: per_device(): call(functools.partial(row_kernel, blocks, own_blocks), sds((tgt_size, 4,...]
  transfers between devices with their start and end apart: 6 -> 5, of which waited for: 4 -> 5; matrix products, arithmetic and copies ran while one was open for 2% -> 1% of each run, Pallas kernels for 10% -> 4%
where the time goes in v4:
time: 120 us; the launch traced here: 119 us
  waiting for transfers between devices  34.5 us (29%)
  blocking collectives  31.4 us (26%)
  starting transfers between devices  28.4 us (24%)
  Pallas kernels  21 us (18%)
  local copies, waits for them, and re-layouts  2.72 us (2%)
    all_to_all x4, waiting for transfers between devices, swap(): return lax.all_to_all(x, axis, 0, 0, tiled=True)  32.9 us
    all_to_all x2, blocking collectives, swap(): return lax.all_to_all(x, axis, 0, 0, tiled=True)  31.4 us
    all_to_all x4, starting transfers between devices, swap(): return lax.all_to_all(x, axis, 0, 0, tiled=True)  22.9 us
    pallas_call x1, Pallas kernels, per_device(): call(functools.partial(row_kernel, blocks, own_blocks), sds((tgt_size, 4,...  6.86 us
    pallas_call x1, Pallas kernels, per_device(): call(functools.partial(column_kernel, blocks, own_blocks), sds((src_size,...  6.12 us
    ppermute x1, starting transfers between devices, per_device(): other = lax.ppermute(mine, TGT[1], [(0, 1), (1, 0)])  5.59 us
    pallas_call x1, Pallas kernels, per_device(): call(functools.partial(listing_kernel, blocks, own_blocks), (sds((slots,)...  4.25 us
  transfers between devices with their start and end apart: 5, of which 5 were waited for; matrix products, arithmetic and copies ran while one was open for 1% of the time, Pallas kernels for 4%

profile of v4, /device:TPU:1, one launch (start us, length us, event | category | flops | bytes accessed | tf_op | source)
XLA Modules:
  0.0 119.5 jit_solution(10213339154899588396)
XLA Ops:
  0.6 0.0 copy-start.2
  0.6 0.0 copy-start.3
  0.7 0.0 copy-start.4
  0.7 0.9 fusion
  1.6 0.1 copy.10
  1.7 0.9 broadcast_in_dim.2
  2.6 7.7 %all-to-all-start = ((bf16[8,256,128]{2,1,0:T(8,128)(2,1)}), bf16[8,256,128]{2,1,0:T(8,128)(2,1)S(1)}, u32[]{:S(2)}, u32[]{:S(2)}) async-start(bf16[8,256,128]{2,1,0:T(8,128)(2,1)} %broadcast_in_dim.2), calls=%async_computation | async-start | bytes 1048576 | tf_op jit(solution)/shard_map/all_to_all | solution.py:60
  10.2 0.8 copy.11.block_map
  11.0 0.1 pad_add_fusion.rank
  11.1 0.0 copy-done.2
  11.1 0.7 shard_map.94.columns
  11.8 0.0 copy-done.3
  11.8 4.3 %shard_map.95 = (s32[648]{0:T(1024)S(1)}, s32[1]{0:T(128)}) custom-call(s32[2]{0:T(128)S(1)} %pad_add_fusion.rank, s32[32,20]{1,0:T(8,128)S(1)} %copy.11.block_map, s32[32]{0:T(128)S(1)} %copy-done.3), custom_call_target="tpu_custom_call" | custom-call | tf_op jit(solution)/shard_map/pallas_call | solution.py:371
  16.1 8.9 %all-to-all-done.mine = bf16[8,256,128]{2,1,0:T(8,128)(2,1)S(1)} async-done(((bf16[8,256,128]{2,1,0:T(8,128)(2,1)}), bf16[8,256,128]{2,1,0:T(8,128)(2,1)S(1)}, u32[]{:S(2)}, u32[]{:S(2)}) %all-to-all-start) | async-done | bytes 524320 | tf_op jit(solution)/shard_map/all_to_all | solution.py:60
  25.0 5.6 %collective-permute-start = (bf16[8,256,128]{2,1,0:T(8,128)(2,1)S(1)}, bf16[8,256,128]{2,1,0:T(8,128)(2,1)S(1)}, u32[]{:S(2)}, u32[]{:S(2)}) collective-permute-start(bf16[8,256,128]{2,1,0:T(8,128)(2,1)S(1)} %all-to-all-done.mine), channel_id=1, source_target_pairs={{0,1},{1,0},{2,3},{3,2},{4,5},{5,4},{6,7},{7,6},{8,9},{9,8},{10,11... | collective-permute-start | bytes 1572872 | tf_op jit(solution)/shard_map/ppermute | solution.py:379
  30.6 1.5 %collective-permute-done.other = bf16[8,256,128]{2,1,0:T(8,128)(2,1)S(1)} collective-permute-done((bf16[8,256,128]{2,1,0:T(8,128)(2,1)S(1)}, bf16[8,256,128]{2,1,0:T(8,128)(2,1)S(1)}, u32[]{:S(2)}, u32[]{:S(2)}) %collective-permute-start) | collective-permute-done | bytes 524320 | tf_op jit(solution)/shard_map/ppermute | solution.py:379
  32.1 0.0 copy-done.4
  32.1 0.0 copy-start
  32.1 6.1 %shard_map.96 = f32[32,4,128]{2,1,0:T(4,128)S(1)} custom-call(s32[648]{0:T(1024)S(1)} %get-tuple-element.14.listed, s32[1]{0:T(128)} %get-tuple-element.15.total, bf16[8,256,128]{2,1,0:T(8,128)(2,1)S(1)} %all-to-all-done.mine, bf16[8,256,128]{2,1,0:T(8,128)(2,1)S(1)} %collective-permute-done.other, bf16[64,16384]{1,0:T(8,128)(2,1)S(1)} %bitcast.8, ...), custom_call_target="tpu_custom_call" | custom-call | flops 10000000000 | bytes 1000000 | tf_op jit(solution)/shard_map/pallas_call | solution.py:390
  38.2 21.5 %all_to_all.30.arrived = f32[32,4,128]{2,1,0:T(4,128)S(1)} all-to-all(f32[32,4,128]{2,1,0:T(4,128)S(1)} %shard_map.96), channel_id=1, replica_groups=mesh['src_0'=4,'src_1'=8,'tgt_0'=8,'tgt_1'=2] {'src_0','src_1'}, dimensions={0} | all-to-all | bytes 131072 | tf_op jit(solution)/shard_map/all_to_all | solution.py:60
  59.8 0.7 shard_map.97
  60.5 3.9 %all-to-all-start.2 = ((f32[32,4,128]{2,1,0:T(4,128)}), f32[32,4,128]{2,1,0:T(4,128)S(1)}, u32[]{:S(2)}, u32[]{:S(2)}) async-start(f32[32,4,128]{2,1,0:T(4,128)} %shard_map.97), calls=%async_computation.2 | async-start | bytes 131072 | tf_op jit(solution)/shard_map/all_to_all | solution.py:60
  64.4 0.0 copy-done
  64.4 0.0 copy-start.1
  64.4 8.8 %all-to-all-done.2.level = f32[32,4,128]{2,1,0:T(4,128)S(1)} async-done(((f32[32,4,128]{2,1,0:T(4,128)}), f32[32,4,128]{2,1,0:T(4,128)S(1)}, u32[]{:S(2)}, u32[]{:S(2)}) %all-to-all-start.2) | async-done | bytes 65568 | tf_op jit(solution)/shard_map/all_to_all | solution.py:60
  73.2 6.9 %shard_map.98 = f32[16,4,128]{2,1,0:T(4,128)} custom-call(s32[2]{0:T(128)S(1)} %pad_add_fusion.rank, s32[648]{0:T(1024)S(1)} %get-tuple-element.14.listed, s32[1]{0:T(128)} %get-tuple-element.15.total, bf16[8,256,128]{2,1,0:T(8,128)(2,1)S(1)} %all-to-all-done.mine, bf16[8,256,128]{2,1,0:T(8,128)(2,1)S(1)} %collective-permute-done.other, ...), custom_call_target="tpu_custom_call" | custom-call | flops 10000000000 | bytes 1000000 | tf_op jit(solution)/shard_map/pallas_call | solution.py:410
  80.1 6.8 %all-to-all-start.3 = ((f32[16,4,128]{2,1,0:T(4,128)}), f32[16,4,128]{2,1,0:T(4,128)S(1)}, u32[]{:S(2)}, u32[]{:S(2)}) async-start(f32[16,4,128]{2,1,0:T(4,128)} %shard_map.98), calls=%async_computation.3 | async-start | bytes 65536 | tf_op jit(solution)/shard_map/all_to_all | solution.py:60
  86.8 0.0 copy-done.1
  86.9 0.2 shard_map.99.moments
  87.1 7.2 %all-to-all-done.3.arrived = f32[16,4,128]{2,1,0:T(4,128)S(1)} async-done(((f32[16,4,128]{2,1,0:T(4,128)}), f32[16,4,128]{2,1,0:T(4,128)S(1)}, u32[]{:S(2)}, u32[]{:S(2)}) %all-to-all-start.3) | async-done | bytes 32800 | tf_op jit(solution)/shard_map/all_to_all | solution.py:60
  94.3 0.6 shard_map.100
  94.9 9.8 %all_to_all.31.arrived = f32[16,1,128]{2,1,0:T(1,128)S(1)} all-to-all(f32[16,1,128]{2,1,0:T(1,128)S(1)} %get-tuple-element.19), channel_id=1, replica_groups=mesh['src_0'=4,'src_1'=8,'tgt_0'=8,'tgt_1'=2] {'tgt_0','tgt_1'}, dimensions={0} | all-to-all | bytes 16384 | tf_op jit(solution)/shard_map/all_to_all | solution.py:60
  104.7 0.6 shard_map.101
  105.4 4.6 %all-to-all-start.5 = ((f32[32,1,128]{2,1,0:T(1,128)}), f32[32,1,128]{2,1,0:T(1,128)S(1)}, u32[]{:S(2)}, u32[]{:S(2)}) async-start(f32[32,1,128]{2,1,0:T(1,128)} %shard_map.101), calls=%async_computation.5 | async-start | bytes 32768 | tf_op jit(solution)/shard_map/all_to_all | solution.py:60
  110.0 0.6 broadcast_multiply_fusion
  110.6 8.0 %all-to-all-done.5.arrived = f32[32,1,128]{2,1,0:T(1,128)S(1)} async-done(((f32[32,1,128]{2,1,0:T(1,128)}), f32[32,1,128]{2,1,0:T(1,128)S(1)}, u32[]{:S(2)}, u32[]{:S(2)}) %all-to-all-start.5) | async-done | bytes 16416 | tf_op jit(solution)/shard_map/all_to_all | solution.py:60
  118.6 0.9 shard_map.102
  (3 shorter events, 0.0 us)
Async XLA Ops:
  0.6 10.5 %copy-start.2 = (f32[8192]{0:T(1024)S(1)}, f32[8192]{0:T(1024)}, u32[]{:S(2)}) copy-start(f32[8192]{0:T(1024)} %param.9) | copy-start | bytes 98308
  0.6 11.2 %copy-start.3 = (s32[32]{0:T(128)S(1)}, s32[32]{0:T(128)}, u32[]{:S(2)}) copy-start(s32[32]{0:T(128)} %counts.1) | copy-start | bytes 388
  0.7 31.5 %copy-start.4 = (bf16[16384,64]{0,1:T(8,128)(2,1)S(1)}, bf16[16384,64]{0,1:T(8,128)(2,1)}, u32[]{:S(2)}) copy-start(bf16[16384,64]{0,1:T(8,128)(2,1)} %param.8) | copy-start | bytes 6291460
  2.6 22.4 %all-to-all-start = ((bf16[8,256,128]{2,1,0:T(8,128)(2,1)}), bf16[8,256,128]{2,1,0:T(8,128)(2,1)S(1)}, u32[]{:S(2)}, u32[]{:S(2)}) async-start(bf16[8,256,128]{2,1,0:T(8,128)(2,1)} %broadcast_in_dim.2), calls=%async_computation | async-start | bytes 1048576 | tf_op jit(solution)/shard_map/all_to_all | solution.py:60
  25.0 7.1 %collective-permute-start = (bf16[8,256,128]{2,1,0:T(8,128)(2,1)S(1)}, bf16[8,256,128]{2,1,0:T(8,128)(2,1)S(1)}, u32[]{:S(2)}, u32[]{:S(2)}) collective-permute-start(bf16[8,256,128]{2,1,0:T(8,128)(2,1)S(1)} %all-to-all-done.mine), channel_id=1, source_target_pairs={{0,1},{1,0},{2,3},{3,2},{4,5},{5,4},{6,7},{7,6},{8,9},{9,8},{10,11... | collective-permute-start | bytes 1572872 | tf_op jit(solution)/shard_map/ppermute | solution.py:379
  32.1 32.2 %copy-start = (f32[8,512]{1,0:T(8,128)S(1)}, f32[8,512]{1,0:T(8,128)}, u32[]{:S(2)}) copy-start(f32[8,512]{1,0:T(8,128)} %steps.1) | copy-start | bytes 49156
  60.5 12.7 %all-to-all-start.2 = ((f32[32,4,128]{2,1,0:T(4,128)}), f32[32,4,128]{2,1,0:T(4,128)S(1)}, u32[]{:S(2)}, u32[]{:S(2)}) async-start(f32[32,4,128]{2,1,0:T(4,128)} %shard_map.97), calls=%async_computation.2 | async-start | bytes 131072 | tf_op jit(solution)/shard_map/all_to_all | solution.py:60
  64.4 22.5 %copy-start.1 = (f32[8,512]{1,0:T(8,128)S(1)}, f32[8,512]{1,0:T(8,128)}, u32[]{:S(2)}) copy-start(f32[8,512]{1,0:T(8,128)} %slopes.1) | copy-start | bytes 49156
  80.1 14.2 %all-to-all-start.3 = ((f32[16,4,128]{2,1,0:T(4,128)}), f32[16,4,128]{2,1,0:T(4,128)S(1)}, u32[]{:S(2)}, u32[]{:S(2)}) async-start(f32[16,4,128]{2,1,0:T(4,128)} %shard_map.98), calls=%async_computation.3 | async-start | bytes 65536 | tf_op jit(solution)/shard_map/all_to_all | solution.py:60
  105.4 13.2 %all-to-all-start.5 = ((f32[32,1,128]{2,1,0:T(1,128)}), f32[32,1,128]{2,1,0:T(1,128)S(1)}, u32[]{:S(2)}, u32[]{:S(2)}) async-start(f32[32,1,128]{2,1,0:T(1,128)} %shard_map.101), calls=%async_computation.5 | async-start | bytes 32768 | tf_op jit(solution)/shard_map/all_to_all | solution.py:60

commit v5 on v4

--- a/solution.py
+++ b/solution.py
@@ -62,6 +62,17 @@
 
 def share(x, axis):
     return swap(jnp.broadcast_to(x[None], (lax.axis_size(axis), *x.shape)), axis)
+
+
+def pack_kernel(given, out):
+    for h in range(BLOCK // HALF):
+        parts = [
+            jnp.transpose(given[:, b * BLOCK + h * HALF : b * BLOCK + (h + 1) * HALF])
+            for b in range(2)
+        ]
+        tile = jnp.concatenate(parts, axis=1)
+        for k in range(out.shape[0]):
+            out[k, h * HALF : (h + 1) * HALF, :] = tile
 
 
 def listing_kernel(blocks, own_blocks, rank, block_map, counts, pairs, total):
@@ -355,8 +366,15 @@
     pieces = sources.shape[0] // BLOCK
     assert pieces == 2
 
-    packed = jnp.concatenate([sources[:BLOCK], sources[BLOCK:]], axis=1)
-    mine = share(packed, TGT[0])
+    packed = call(
+        pack_kernel,
+        sds((lax.axis_size(TGT[0]), BLOCK, HALF), jnp.bfloat16),
+        [VMEM],
+        VMEM,
+        (),
+        COST,
+    )(sources.T)
+    mine = swap(packed, TGT[0])
     core = lax.axis_index(TGT[1])
     t = targets.T
     rank = jnp.stack([lax.axis_index(TGT), core]).astype(jnp.int32)
@@ -375,8 +393,6 @@
         [SMEM] * 2,
     )(rank, block_map, counts)
 
-    mine, columns, pairs, total = lax.optimization_barrier((mine, columns, pairs, total))
-    other = lax.ppermute(mine, TGT[1], [(0, 1), (1, 0)])
     history = jnp.concatenate([step_history, slope_history], axis=0)
     moments = call(
         functools.partial(moments_kernel, stored),
@@ -385,7 +401,10 @@
         VMEM,
         [pltpu.VMEM((2 * stored, HALF), F32)],
     )(history)
-
+    mine, columns, pairs, total, moments = lax.optimization_barrier(
+        (mine, columns, pairs, total, moments)
+    )
+    other = lax.ppermute(mine, TGT[1], [(0, 1), (1, 0)])
     rows = pltpu.VMEM((blocks, BLOCK, HALF), jnp.bfloat16)
     levels = call(
         functools.partial(column_kernel, blocks, own_blocks),
@@ -420,13 +439,14 @@
         COST,
     )(rank, pairs, total, mine, other, t, columns, level)
 
+    arrived, target_potential = lax.optimization_barrier((swap(parts, TGT), target_potential))
     ratio = blocks * src_size / (own_blocks * tgt_size)
     gradient, again, dots = call(
         functools.partial(gradient_kernel, tgt_size, ratio),
         (sds((4, HALF)), sds((4, HALF)), sds((tgt_size, 1, HALF))),
         [VMEM] * 3,
         [VMEM] * 3,
-    )(swap(parts, TGT), history, moments)
+    )(arrived, history, moments)
     dots = call(pass_on_kernel, sds((src_size, 1, HALF)), [VMEM], VMEM)(swap(dots, TGT))
     direction = call(
         functools.partial(direction_kernel, src_size, stored), sds((4, HALF)), [VMEM] * 4, VMEM

time: 120 us -> 117 us (0.975)
  blocking collectives: 31.4 us -> 56.1 us
  waiting for transfers between devices: 34.5 us -> 17.7 us
  starting transfers between devices: 28.4 us -> 21.3 us
  local copies, waits for them, and re-layouts: 2.72 us -> 0.95 us
  Pallas kernels: 21 us -> 19.6 us
    all_to_all x2 -> x4, blocking collectives: 31.4 us -> 56.1 us  [swap(): return lax.all_to_all(x, axis, 0, 0, tiled=True)]
    all_to_all x4 -> x2, waiting for transfers between devices: 32.9 us -> 16.2 us  [swap(): return lax.all_to_all(x, axis, 0, 0, tiled=True)]
    all_to_all x4 -> x2, starting transfers between devices: 22.9 us -> 15.7 us  [swap(): return lax.all_to_all(x, axis, 0, 0, tiled=True)]
  transfers between devices with their start and end apart: 5 -> 3, of which waited for: 5 -> 3; matrix products, arithmetic and copies ran while one was open for 1% -> 1% of each run, Pallas kernels for 4% -> 4%
where the time goes in v5:
time: 117 us
  blocking collectives  56.1 us (48%)
  starting transfers between devices  21.3 us (18%)
  Pallas kernels  19.6 us (17%)
  waiting for transfers between devices  17.7 us (15%)
    all_to_all x4, blocking collectives, swap(): return lax.all_to_all(x, axis, 0, 0, tiled=True)  56.1 us
    all_to_all x2, waiting for transfers between devices, swap(): return lax.all_to_all(x, axis, 0, 0, tiled=True)  16.2 us
    all_to_all x2, starting transfers between devices, swap(): return lax.all_to_all(x, axis, 0, 0, tiled=True)  15.7 us
    pallas_call x1, Pallas kernels, per_device(): call(functools.partial(row_kernel, blocks, own_blocks), sds((tgt_size, 4,...  6.4 us
    ppermute x1, starting transfers between devices, per_device(): other = lax.ppermute(mine, TGT[1], [(0, 1), (1, 0)])  5.59 us
    pallas_call x1, Pallas kernels, per_device(): call(functools.partial(column_kernel, blocks, own_blocks), sds((src_size,...  5.41 us
    pallas_call x1, Pallas kernels, per_device(): call(functools.partial(listing_kernel, blocks, own_blocks), (sds((slots,)...  4.25 us
  transfers between devices with their start and end apart: 3, of which 3 were waited for; matrix products, arithmetic and copies ran while one was open for 1% of the time, Pallas kernels for 4%

profile of v5, /device:TPU:1, one launch (start us, length us, event | category | flops | bytes accessed | tf_op | source)
XLA Modules:
  0.0 117.0 jit_solution(4528177159746609500)
XLA Ops:
  0.6 0.0 copy-start.5
  0.6 0.8 copy-done.5
  1.5 0.0 copy-start.6
  1.5 0.0 copy-start
  1.5 0.0 copy-start.1
  1.5 0.0 copy-start.2
  1.5 0.0 copy-start.3
  1.5 0.0 copy-start.4
  1.5 1.0 shard_map.94
  2.5 7.7 %all-to-all-start = ((bf16[8,256,128]{2,1,0:T(8,128)(2,1)}), bf16[8,256,128]{2,1,0:T(8,128)(2,1)S(1)}, u32[]{:S(2)}, u32[]{:S(2)}) async-start(bf16[8,256,128]{2,1,0:T(8,128)(2,1)} %shard_map.94), calls=%async_computation | async-start | bytes 1048576 | tf_op jit(solution)/shard_map/all_to_all | solution.py:60
  10.1 0.0 copy-done.6
  10.1 0.1 copy.10.block_map
  10.2 0.0 copy-done
  10.2 0.0 copy-done.1
  10.3 0.2 shard_map.97.moments
  10.5 0.1 pad_add_fusion.rank
  10.6 0.0 copy-done.2
  10.6 0.7 shard_map.95.columns
  11.3 0.0 copy-done.3
  11.3 4.3 %shard_map.96 = (s32[648]{0:T(1024)S(1)}, s32[1]{0:T(128)}) custom-call(s32[2]{0:T(128)S(1)} %pad_add_fusion.rank, s32[32,20]{1,0:T(8,128)S(1)} %copy.10.block_map, s32[32]{0:T(128)S(1)} %copy-done.3), custom_call_target="tpu_custom_call" | custom-call | tf_op jit(solution)/shard_map/pallas_call | solution.py:389
  15.6 9.3 %all-to-all-done.mine = bf16[8,256,128]{2,1,0:T(8,128)(2,1)S(1)} async-done(((bf16[8,256,128]{2,1,0:T(8,128)(2,1)}), bf16[8,256,128]{2,1,0:T(8,128)(2,1)S(1)}, u32[]{:S(2)}, u32[]{:S(2)}) %all-to-all-start) | async-done | bytes 524320 | tf_op jit(solution)/shard_map/all_to_all | solution.py:60
  24.9 5.6 %collective-permute-start = (bf16[8,256,128]{2,1,0:T(8,128)(2,1)S(1)}, bf16[8,256,128]{2,1,0:T(8,128)(2,1)S(1)}, u32[]{:S(2)}, u32[]{:S(2)}) collective-permute-start(bf16[8,256,128]{2,1,0:T(8,128)(2,1)S(1)} %all-to-all-done.mine), channel_id=1, source_target_pairs={{0,1},{1,0},{2,3},{3,2},{4,5},{5,4},{6,7},{7,6},{8,9},{9,8},{10,11... | collective-permute-start | bytes 1572872 | tf_op jit(solution)/shard_map/ppermute | solution.py:407
  30.5 1.5 %collective-permute-done.other = bf16[8,256,128]{2,1,0:T(8,128)(2,1)S(1)} collective-permute-done((bf16[8,256,128]{2,1,0:T(8,128)(2,1)S(1)}, bf16[8,256,128]{2,1,0:T(8,128)(2,1)S(1)}, u32[]{:S(2)}, u32[]{:S(2)}) %collective-permute-start) | collective-permute-done | bytes 524320 | tf_op jit(solution)/shard_map/ppermute | solution.py:407
  32.0 0.0 copy-done.4
  32.0 5.4 %shard_map.98 = f32[32,4,128]{2,1,0:T(4,128)S(1)} custom-call(s32[648]{0:T(1024)S(1)} %get-tuple-element.17.listed, s32[1]{0:T(128)} %get-tuple-element.18.total, bf16[8,256,128]{2,1,0:T(8,128)(2,1)S(1)} %all-to-all-done.mine, bf16[8,256,128]{2,1,0:T(8,128)(2,1)S(1)} %collective-permute-done.other, bf16[64,16384]{1,0:T(8,128)(2,1)S(1)} %bitcast.9, ...), custom_call_target="tpu_custom_call" | custom-call | flops 10000000000 | bytes 1000000 | tf_op jit(solution)/shard_map/pallas_call | solution.py:409
  37.4 22.3 %all_to_all.30.arrived = f32[32,4,128]{2,1,0:T(4,128)S(1)} all-to-all(f32[32,4,128]{2,1,0:T(4,128)S(1)} %shard_map.98), channel_id=1, replica_groups=mesh['src_0'=4,'src_1'=8,'tgt_0'=8,'tgt_1'=2] {'src_0','src_1'}, dimensions={0} | all-to-all | bytes 131072 | tf_op jit(solution)/shard_map/all_to_all | solution.py:60
  59.7 0.1 shard_map.99
  59.8 11.9 %all_to_all.31.level = f32[32,4,128]{2,1,0:T(4,128)S(1)} all-to-all(f32[32,4,128]{2,1,0:T(4,128)S(1)} %shard_map.99), channel_id=1, replica_groups=mesh['src_0'=4,'src_1'=8,'tgt_0'=8,'tgt_1'=2] {'src_0','src_1'}, dimensions={0} | all-to-all | bytes 131072 | tf_op jit(solution)/shard_map/all_to_all | solution.py:60
  71.7 6.4 %shard_map.100 = f32[16,4,128]{2,1,0:T(4,128)} custom-call(s32[2]{0:T(128)S(1)} %pad_add_fusion.rank, s32[648]{0:T(1024)S(1)} %get-tuple-element.17.listed, s32[1]{0:T(128)} %get-tuple-element.18.total, bf16[8,256,128]{2,1,0:T(8,128)(2,1)S(1)} %all-to-all-done.mine, bf16[8,256,128]{2,1,0:T(8,128)(2,1)S(1)} %collective-permute-done.other, ...), custom_call_target="tpu_custom_call" | custom-call | flops 10000000000 | bytes 1000000 | tf_op jit(solution)/shard_map/pallas_call | solution.py:429
  78.2 8.0 %all-to-all-start.3 = ((f32[16,4,128]{2,1,0:T(4,128)}), f32[16,4,128]{2,1,0:T(4,128)S(1)}, u32[]{:S(2)}, u32[]{:S(2)}) async-start(f32[16,4,128]{2,1,0:T(4,128)} %shard_map.100), calls=%async_computation.3 | async-start | bytes 65536 | tf_op jit(solution)/shard_map/all_to_all | solution.py:60
  86.2 0.6 broadcast_multiply_fusion
  86.8 6.8 %all-to-all-done.3.arrived = f32[16,4,128]{2,1,0:T(4,128)S(1)} async-done(((f32[16,4,128]{2,1,0:T(4,128)}), f32[16,4,128]{2,1,0:T(4,128)S(1)}, u32[]{:S(2)}, u32[]{:S(2)}) %all-to-all-start.3) | async-done | bytes 32800 | tf_op jit(solution)/shard_map/all_to_all | solution.py:60
  93.7 0.6 shard_map.101
  94.3 9.8 %all_to_all.32.arrived = f32[16,1,128]{2,1,0:T(1,128)S(1)} all-to-all(f32[16,1,128]{2,1,0:T(1,128)S(1)} %get-tuple-element.24), channel_id=1, replica_groups=mesh['src_0'=4,'src_1'=8,'tgt_0'=8,'tgt_1'=2] {'tgt_0','tgt_1'}, dimensions={0} | all-to-all | bytes 16384 | tf_op jit(solution)/shard_map/all_to_all | solution.py:60
  104.1 12.0 %all_to_all.33.arrived = f32[32,1,128]{2,1,0:T(1,128)S(1)} all-to-all(f32[32,1,128]{2,1,0:T(1,128)S(1)} %shard_map.102), channel_id=1, replica_groups=mesh['src_0'=4,'src_1'=8,'tgt_0'=8,'tgt_1'=2] {'src_0','src_1'}, dimensions={0} | all-to-all | bytes 32768 | tf_op jit(solution)/shard_map/all_to_all | solution.py:60
  116.1 0.9 shard_map.103
  (3 shorter events, 0.0 us)
Async XLA Ops:
  0.6 0.8 copy-start.5
  1.5 8.7 %copy-start.6 = (s32[32,20]{0,1:T(8,128)S(1)}, s32[32,20]{0,1:T(8,128)}, u32[]{:S(2)}) copy-start(s32[32,20]{0,1:T(8,128)} %param.10) | copy-start | bytes 7684
  1.5 8.8 %copy-start = (f32[8,512]{1,0:T(8,128)S(1)}, f32[8,512]{1,0:T(8,128)}, u32[]{:S(2)}) copy-start(f32[8,512]{1,0:T(8,128)} %steps.1) | copy-start | bytes 49156
  1.5 8.8 %copy-start.1 = (f32[8,512]{1,0:T(8,128)S(1)}, f32[8,512]{1,0:T(8,128)}, u32[]{:S(2)}) copy-start(f32[8,512]{1,0:T(8,128)} %slopes.1) | copy-start | bytes 49156
  1.5 9.1 %copy-start.2 = (f32[8192]{0:T(1024)S(1)}, f32[8192]{0:T(1024)}, u32[]{:S(2)}) copy-start(f32[8192]{0:T(1024)} %param.9) | copy-start | bytes 98308
  1.5 9.8 %copy-start.3 = (s32[32]{0:T(128)S(1)}, s32[32]{0:T(128)}, u32[]{:S(2)}) copy-start(s32[32]{0:T(128)} %counts.1) | copy-start | bytes 388
  1.5 30.5 %copy-start.4 = (bf16[16384,64]{0,1:T(8,128)(2,1)S(1)}, bf16[16384,64]{0,1:T(8,128)(2,1)}, u32[]{:S(2)}) copy-start(bf16[16384,64]{0,1:T(8,128)(2,1)} %param.8) | copy-start | bytes 6291460
  2.5 22.4 %all-to-all-start = ((bf16[8,256,128]{2,1,0:T(8,128)(2,1)}), bf16[8,256,128]{2,1,0:T(8,128)(2,1)S(1)}, u32[]{:S(2)}, u32[]{:S(2)}) async-start(bf16[8,256,128]{2,1,0:T(8,128)(2,1)} %shard_map.94), calls=%async_computation | async-start | bytes 1048576 | tf_op jit(solution)/shard_map/all_to_all | solution.py:60
  24.9 7.1 %collective-permute-start = (bf16[8,256,128]{2,1,0:T(8,128)(2,1)S(1)}, bf16[8,256,128]{2,1,0:T(8,128)(2,1)S(1)}, u32[]{:S(2)}, u32[]{:S(2)}) collective-permute-start(bf16[8,256,128]{2,1,0:T(8,128)(2,1)S(1)} %all-to-all-done.mine), channel_id=1, source_target_pairs={{0,1},{1,0},{2,3},{3,2},{4,5},{5,4},{6,7},{7,6},{8,9},{9,8},{10,11... | collective-permute-start | bytes 1572872 | tf_op jit(solution)/shard_map/ppermute | solution.py:407
  78.2 15.5 %all-to-all-start.3 = ((f32[16,4,128]{2,1,0:T(4,128)}), f32[16,4,128]{2,1,0:T(4,128)S(1)}, u32[]{:S(2)}, u32[]{:S(2)}) async-start(f32[16,4,128]{2,1,0:T(4,128)} %shard_map.100), calls=%async_computation.3 | async-start | bytes 65536 | tf_op jit(solution)/shard_map/all_to_all | solution.py:60

commit v6 on v5

--- a/solution.py
+++ b/solution.py
@@ -18,7 +18,7 @@
 LN2 = 0.6931471805599453
 entropy = 0.5
 SCALE = LOG2E / entropy
-UNROLL = 8
+UNROLL = 12
 PLACE = 1 << 16
 WIDE = 64
 F32 = jnp.float32

time: 117 us -> 118 us (level)
  Pallas kernels: 19.6 us -> 21.3 us
where the time goes in v6:
time: 118 us; the launch traced here: 117 us
  blocking collectives  55.6 us (47%)
  Pallas kernels  21.3 us (18%)
  starting transfers between devices  20.4 us (17%)
  waiting for transfers between devices  17.6 us (15%)
    all_to_all x4, blocking collectives, swap(): return lax.all_to_all(x, axis, 0, 0, tiled=True)  55.6 us
    all_to_all x2, waiting for transfers between devices, swap(): return lax.all_to_all(x, axis, 0, 0, tiled=True)  16 us
    all_to_all x2, starting transfers between devices, swap(): return lax.all_to_all(x, axis, 0, 0, tiled=True)  14.8 us
    pallas_call x1, Pallas kernels, per_device(): call(functools.partial(row_kernel, blocks, own_blocks), sds((tgt_size, 4,...  6.98 us
    pallas_call x1, Pallas kernels, per_device(): call(functools.partial(column_kernel, blocks, own_blocks), sds((src_size,...  6.58 us
    ppermute x1, starting transfers between devices, per_device(): other = lax.ppermute(mine, TGT[1], [(0, 1), (1, 0)])  5.59 us
    pallas_call x1, Pallas kernels, per_device(): call(functools.partial(listing_kernel, blocks, own_blocks), (sds((slots,)...  4.27 us
  transfers between devices with their start and end apart: 3, of which 3 were waited for; matrix products, arithmetic and copies ran while one was open for 1% of the time, Pallas kernels for 4%

profile of v6, /device:TPU:1, one launch (start us, length us, event | category | flops | bytes accessed | tf_op | source)
XLA Modules:
  0.0 117.3 jit_solution(13196041309883964854)
XLA Ops:
  0.6 0.0 copy-start.5
  0.6 0.8 copy-done.5
  1.5 0.0 copy-start.6
  1.5 0.0 copy-start
  1.5 0.0 copy-start.1
  1.5 0.0 copy-start.2
  1.5 0.0 copy-start.3
  1.5 0.0 copy-start.4
  1.5 1.0 shard_map.94
  2.5 7.7 %all-to-all-start = ((bf16[8,256,128]{2,1,0:T(8,128)(2,1)}), bf16[8,256,128]{2,1,0:T(8,128)(2,1)S(1)}, u32[]{:S(2)}, u32[]{:S(2)}) async-start(bf16[8,256,128]{2,1,0:T(8,128)(2,1)} %shard_map.94), calls=%async_computation | async-start | bytes 1048576 | tf_op jit(solution)/shard_map/all_to_all | solution.py:60
  10.1 0.0 copy-done.6
  10.1 0.1 copy.10.block_map
  10.2 0.0 copy-done
  10.2 0.0 copy-done.1
  10.3 0.2 shard_map.97.moments
  10.5 0.1 pad_add_fusion.rank
  10.6 0.0 copy-done.2
  10.6 0.7 shard_map.95.columns
  11.3 0.0 copy-done.3
  11.3 4.3 %shard_map.96 = (s32[652]{0:T(1024)S(1)}, s32[1]{0:T(128)}) custom-call(s32[2]{0:T(128)S(1)} %pad_add_fusion.rank, s32[32,20]{1,0:T(8,128)S(1)} %copy.10.block_map, s32[32]{0:T(128)S(1)} %copy-done.3), custom_call_target="tpu_custom_call" | custom-call | tf_op jit(solution)/shard_map/pallas_call | solution.py:389
  15.6 9.3 %all-to-all-done.mine = bf16[8,256,128]{2,1,0:T(8,128)(2,1)S(1)} async-done(((bf16[8,256,128]{2,1,0:T(8,128)(2,1)}), bf16[8,256,128]{2,1,0:T(8,128)(2,1)S(1)}, u32[]{:S(2)}, u32[]{:S(2)}) %all-to-all-start) | async-done | bytes 524320 | tf_op jit(solution)/shard_map/all_to_all | solution.py:60
  24.9 5.6 %collective-permute-start = (bf16[8,256,128]{2,1,0:T(8,128)(2,1)S(1)}, bf16[8,256,128]{2,1,0:T(8,128)(2,1)S(1)}, u32[]{:S(2)}, u32[]{:S(2)}) collective-permute-start(bf16[8,256,128]{2,1,0:T(8,128)(2,1)S(1)} %all-to-all-done.mine), channel_id=1, source_target_pairs={{0,1},{1,0},{2,3},{3,2},{4,5},{5,4},{6,7},{7,6},{8,9},{9,8},{10,11... | collective-permute-start | bytes 1572872 | tf_op jit(solution)/shard_map/ppermute | solution.py:407
  30.5 1.5 %collective-permute-done.other = bf16[8,256,128]{2,1,0:T(8,128)(2,1)S(1)} collective-permute-done((bf16[8,256,128]{2,1,0:T(8,128)(2,1)S(1)}, bf16[8,256,128]{2,1,0:T(8,128)(2,1)S(1)}, u32[]{:S(2)}, u32[]{:S(2)}) %collective-permute-start) | collective-permute-done | bytes 524320 | tf_op jit(solution)/shard_map/ppermute | solution.py:407
  32.0 0.0 copy-done.4
  32.0 6.6 %shard_map.98 = f32[32,4,128]{2,1,0:T(4,128)S(1)} custom-call(s32[652]{0:T(1024)S(1)} %get-tuple-element.17.listed, s32[1]{0:T(128)} %get-tuple-element.18.total, bf16[8,256,128]{2,1,0:T(8,128)(2,1)S(1)} %all-to-all-done.mine, bf16[8,256,128]{2,1,0:T(8,128)(2,1)S(1)} %collective-permute-done.other, bf16[64,16384]{1,0:T(8,128)(2,1)S(1)} %bitcast.9, ...), custom_call_target="tpu_custom_call" | custom-call | flops 10000000000 | bytes 1000000 | tf_op jit(solution)/shard_map/pallas_call | solution.py:409
  38.6 20.7 %all_to_all.30.arrived = f32[32,4,128]{2,1,0:T(4,128)S(1)} all-to-all(f32[32,4,128]{2,1,0:T(4,128)S(1)} %shard_map.98), channel_id=1, replica_groups=mesh['src_0'=4,'src_1'=8,'tgt_0'=8,'tgt_1'=2] {'src_0','src_1'}, dimensions={0} | all-to-all | bytes 131072 | tf_op jit(solution)/shard_map/all_to_all | solution.py:60
  59.3 0.1 shard_map.99
  59.4 11.9 %all_to_all.31.level = f32[32,4,128]{2,1,0:T(4,128)S(1)} all-to-all(f32[32,4,128]{2,1,0:T(4,128)S(1)} %shard_map.99), channel_id=1, replica_groups=mesh['src_0'=4,'src_1'=8,'tgt_0'=8,'tgt_1'=2] {'src_0','src_1'}, dimensions={0} | all-to-all | bytes 131072 | tf_op jit(solution)/shard_map/all_to_all | solution.py:60
  71.3 7.0 %shard_map.100 = f32[16,4,128]{2,1,0:T(4,128)} custom-call(s32[2]{0:T(128)S(1)} %pad_add_fusion.rank, s32[652]{0:T(1024)S(1)} %get-tuple-element.17.listed, s32[1]{0:T(128)} %get-tuple-element.18.total, bf16[8,256,128]{2,1,0:T(8,128)(2,1)S(1)} %all-to-all-done.mine, bf16[8,256,128]{2,1,0:T(8,128)(2,1)S(1)} %collective-permute-done.other, ...), custom_call_target="tpu_custom_call" | custom-call | flops 10000000000 | bytes 1000000 | tf_op jit(solution)/shard_map/pallas_call | solution.py:429
  78.2 7.2 %all-to-all-start.3 = ((f32[16,4,128]{2,1,0:T(4,128)}), f32[16,4,128]{2,1,0:T(4,128)S(1)}, u32[]{:S(2)}, u32[]{:S(2)}) async-start(f32[16,4,128]{2,1,0:T(4,128)} %shard_map.100), calls=%async_computation.3 | async-start | bytes 65536 | tf_op jit(solution)/shard_map/all_to_all | solution.py:60
  85.4 0.6 broadcast_multiply_fusion
  86.1 6.7 %all-to-all-done.3.arrived = f32[16,4,128]{2,1,0:T(4,128)S(1)} async-done(((f32[16,4,128]{2,1,0:T(4,128)}), f32[16,4,128]{2,1,0:T(4,128)S(1)}, u32[]{:S(2)}, u32[]{:S(2)}) %all-to-all-start.3) | async-done | bytes 32800 | tf_op jit(solution)/shard_map/all_to_all | solution.py:60
  92.8 0.6 shard_map.101
  93.4 9.8 %all_to_all.32.arrived = f32[16,1,128]{2,1,0:T(1,128)S(1)} all-to-all(f32[16,1,128]{2,1,0:T(1,128)S(1)} %get-tuple-element.24), channel_id=1, replica_groups=mesh['src_0'=4,'src_1'=8,'tgt_0'=8,'tgt_1'=2] {'tgt_0','tgt_1'}, dimensions={0} | all-to-all | bytes 16384 | tf_op jit(solution)/shard_map/all_to_all | solution.py:60
  103.3 13.2 %all_to_all.33.arrived = f32[32,1,128]{2,1,0:T(1,128)S(1)} all-to-all(f32[32,1,128]{2,1,0:T(1,128)S(1)} %shard_map.102), channel_id=1, replica_groups=mesh['src_0'=4,'src_1'=8,'tgt_0'=8,'tgt_1'=2] {'src_0','src_1'}, dimensions={0} | all-to-all | bytes 32768 | tf_op jit(solution)/shard_map/all_to_all | solution.py:60
  116.4 0.9 shard_map.103
  (3 shorter events, 0.0 us)
Async XLA Ops:
  0.6 0.8 copy-start.5
  1.5 8.7 %copy-start.6 = (s32[32,20]{0,1:T(8,128)S(1)}, s32[32,20]{0,1:T(8,128)}, u32[]{:S(2)}) copy-start(s32[32,20]{0,1:T(8,128)} %param.10) | copy-start | bytes 7684
  1.5 8.8 %copy-start = (f32[8,512]{1,0:T(8,128)S(1)}, f32[8,512]{1,0:T(8,128)}, u32[]{:S(2)}) copy-start(f32[8,512]{1,0:T(8,128)} %steps.1) | copy-start | bytes 49156
  1.5 8.8 %copy-start.1 = (f32[8,512]{1,0:T(8,128)S(1)}, f32[8,512]{1,0:T(8,128)}, u32[]{:S(2)}) copy-start(f32[8,512]{1,0:T(8,128)} %slopes.1) | copy-start | bytes 49156
  1.5 9.1 %copy-start.2 = (f32[8192]{0:T(1024)S(1)}, f32[8192]{0:T(1024)}, u32[]{:S(2)}) copy-start(f32[8192]{0:T(1024)} %param.9) | copy-start | bytes 98308
  1.5 9.8 %copy-start.3 = (s32[32]{0:T(128)S(1)}, s32[32]{0:T(128)}, u32[]{:S(2)}) copy-start(s32[32]{0:T(128)} %counts.1) | copy-start | bytes 388
  1.5 30.5 %copy-start.4 = (bf16[16384,64]{0,1:T(8,128)(2,1)S(1)}, bf16[16384,64]{0,1:T(8,128)(2,1)}, u32[]{:S(2)}) copy-start(bf16[16384,64]{0,1:T(8,128)(2,1)} %param.8) | copy-start | bytes 6291460
  2.5 22.4 %all-to-all-start = ((bf16[8,256,128]{2,1,0:T(8,128)(2,1)}), bf16[8,256,128]{2,1,0:T(8,128)(2,1)S(1)}, u32[]{:S(2)}, u32[]{:S(2)}) async-start(bf16[8,256,128]{2,1,0:T(8,128)(2,1)} %shard_map.94), calls=%async_computation | async-start | bytes 1048576 | tf_op jit(solution)/shard_map/all_to_all | solution.py:60
  24.9 7.1 %collective-permute-start = (bf16[8,256,128]{2,1,0:T(8,128)(2,1)S(1)}, bf16[8,256,128]{2,1,0:T(8,128)(2,1)S(1)}, u32[]{:S(2)}, u32[]{:S(2)}) collective-permute-start(bf16[8,256,128]{2,1,0:T(8,128)(2,1)S(1)} %all-to-all-done.mine), channel_id=1, source_target_pairs={{0,1},{1,0},{2,3},{3,2},{4,5},{5,4},{6,7},{7,6},{8,9},{9,8},{10,11... | collective-permute-start | bytes 1572872 | tf_op jit(solution)/shard_map/ppermute | solution.py:407
  78.2 14.6 %all-to-all-start.3 = ((f32[16,4,128]{2,1,0:T(4,128)}), f32[16,4,128]{2,1,0:T(4,128)S(1)}, u32[]{:S(2)}, u32[]{:S(2)}) async-start(f32[16,4,128]{2,1,0:T(4,128)} %shard_map.100), calls=%async_computation.3 | async-start | bytes 65536 | tf_op jit(solution)/shard_map/all_to_all | solution.py:60

commit v7 on v6

--- a/solution.py
+++ b/solution.py
@@ -227,17 +227,13 @@
     rank,
     listed,
     total,
-    mine,
-    other,
+    x,
     t,
-    columns,
     level,
     out,
-    x,
     acc,
     sums,
 ):
-    lay_out(mine, other, columns, x)
     acc[...] = jnp.zeros(acc.shape, F32)
     live = total[0]
     row = lax.broadcasted_iota(jnp.int32, (16, HALF), 0)
@@ -281,7 +277,7 @@
     core = rank[1]
     place = 0
     for side in (core, 1 - core):
-        for y in range(mine.shape[0]):
+        for y in range(blocks // 4):
             out[2 * y + side] = sums[place]
             place += 1
 
@@ -405,13 +401,12 @@
         (mine, columns, pairs, total, moments)
     )
     other = lax.ppermute(mine, TGT[1], [(0, 1), (1, 0)])
-    rows = pltpu.VMEM((blocks, BLOCK, HALF), jnp.bfloat16)
-    levels = call(
+    levels, x = call(
         functools.partial(column_kernel, blocks, own_blocks),
-        sds((src_size, 4, HALF)),
+        (sds((src_size, 4, HALF)), sds((blocks, BLOCK, HALF), jnp.bfloat16)),
         [SMEM] * 2 + [VMEM] * 4,
-        VMEM,
-        [rows] + [pltpu.VMEM((8 * own_blocks + 8, BLOCK), F32)] * 2,
+        [VMEM] * 2,
+        [pltpu.VMEM((8 * own_blocks + 8, BLOCK), F32)] * 2,
         COST,
     )(pairs, total, mine, other, t, columns)
 
@@ -429,15 +424,14 @@
     parts = call(
         functools.partial(row_kernel, blocks, own_blocks),
         sds((tgt_size, 4, HALF)),
-        [SMEM] * 3 + [VMEM] * 5,
+        [SMEM] * 3 + [VMEM] * 3,
         VMEM,
         [
-            rows,
             pltpu.VMEM((blocks + 1, BLOCK, HALF), F32),
             pltpu.VMEM((tgt_size, 4, HALF), F32),
         ],
         COST,
-    )(rank, pairs, total, mine, other, t, columns, level)
+    )(rank, pairs, total, x, t, level)
 
     arrived, target_potential = lax.optimization_barrier((swap(parts, TGT), target_potential))
     ratio = blocks * src_size / (own_blocks * tgt_size)

time: 118 us -> 117 us (level)
  Pallas kernels: 21.3 us -> 19 us
    pallas_call x1, Pallas kernels: 6.98 us -> 5.6 us  [per_device(): call(functools.partial(row_kernel, blocks, own_blocks), sds((tgt_size, 4,...]
where the time goes in v7:
time: 117 us; the launch traced here: 116 us
  blocking collectives  56.1 us (48%)
  starting transfers between devices  21.3 us (18%)
  Pallas kernels  19 us (16%)
  waiting for transfers between devices  17.7 us (15%)
    all_to_all x4, blocking collectives, swap(): return lax.all_to_all(x, axis, 0, 0, tiled=True)  56.1 us
    all_to_all x2, waiting for transfers between devices, swap(): return lax.all_to_all(x, axis, 0, 0, tiled=True)  16.1 us
    all_to_all x2, starting transfers between devices, swap(): return lax.all_to_all(x, axis, 0, 0, tiled=True)  15.7 us
    pallas_call x1, Pallas kernels, per_device(): call(functools.partial(row_kernel, blocks, own_blocks), sds((tgt_size, 4,...  5.6 us
    pallas_call x1, Pallas kernels, per_device(): call(functools.partial(column_kernel, blocks, own_blocks), (sds((src_size...  5.6 us
    ppermute x1, starting transfers between devices, per_device(): other = lax.ppermute(mine, TGT[1], [(0, 1), (1, 0)])  5.59 us
    pallas_call x1, Pallas kernels, per_device(): call(functools.partial(listing_kernel, blocks, own_blocks), (sds((slots,)...  4.27 us
  transfers between devices with their start and end apart: 3, of which 3 were waited for; matrix products, arithmetic and copies ran while one was open for 1% of the time, Pallas kernels for 4%

profile of v7, /device:TPU:1, one launch (start us, length us, event | category | flops | bytes accessed | tf_op | source)
XLA Modules:
  0.0 116.4 jit_solution(6504326320479202789)
XLA Ops:
  0.6 0.0 copy-start.5
  0.6 0.8 copy-done.5
  1.5 0.0 copy-start.6
  1.5 0.0 copy-start
  1.5 0.0 copy-start.1
  1.5 0.0 copy-start.2
  1.5 0.0 copy-start.3
  1.5 0.0 copy-start.4
  1.5 1.0 shard_map.94
  2.5 7.7 %all-to-all-start = ((bf16[8,256,128]{2,1,0:T(8,128)(2,1)}), bf16[8,256,128]{2,1,0:T(8,128)(2,1)S(1)}, u32[]{:S(2)}, u32[]{:S(2)}) async-start(bf16[8,256,128]{2,1,0:T(8,128)(2,1)} %shard_map.94), calls=%async_computation | async-start | bytes 1048576 | tf_op jit(solution)/shard_map/all_to_all | solution.py:60
  10.1 0.0 copy-done.6
  10.1 0.1 copy.10.block_map
  10.2 0.0 copy-done
  10.2 0.0 copy-done.1
  10.2 0.2 shard_map.97.moments
  10.5 0.1 pad_add_fusion.rank
  10.6 0.0 copy-done.2
  10.6 0.7 shard_map.95.columns
  11.3 0.0 copy-done.3
  11.3 4.3 %shard_map.96 = (s32[652]{0:T(1024)S(1)}, s32[1]{0:T(128)}) custom-call(s32[2]{0:T(128)S(1)} %pad_add_fusion.rank, s32[32,20]{1,0:T(8,128)S(1)} %copy.10.block_map, s32[32]{0:T(128)S(1)} %copy-done.3), custom_call_target="tpu_custom_call" | custom-call | tf_op jit(solution)/shard_map/pallas_call | solution.py:385
  15.6 9.3 %all-to-all-done.mine = bf16[8,256,128]{2,1,0:T(8,128)(2,1)S(1)} async-done(((bf16[8,256,128]{2,1,0:T(8,128)(2,1)}), bf16[8,256,128]{2,1,0:T(8,128)(2,1)S(1)}, u32[]{:S(2)}, u32[]{:S(2)}) %all-to-all-start) | async-done | bytes 524320 | tf_op jit(solution)/shard_map/all_to_all | solution.py:60
  24.9 5.6 %collective-permute-start = (bf16[8,256,128]{2,1,0:T(8,128)(2,1)S(1)}, bf16[8,256,128]{2,1,0:T(8,128)(2,1)S(1)}, u32[]{:S(2)}, u32[]{:S(2)}) collective-permute-start(bf16[8,256,128]{2,1,0:T(8,128)(2,1)S(1)} %all-to-all-done.mine), channel_id=1, source_target_pairs={{0,1},{1,0},{2,3},{3,2},{4,5},{5,4},{6,7},{7,6},{8,9},{9,8},{10,11... | collective-permute-start | bytes 1572872 | tf_op jit(solution)/shard_map/ppermute | solution.py:403
  30.5 1.5 %collective-permute-done.other = bf16[8,256,128]{2,1,0:T(8,128)(2,1)S(1)} collective-permute-done((bf16[8,256,128]{2,1,0:T(8,128)(2,1)S(1)}, bf16[8,256,128]{2,1,0:T(8,128)(2,1)S(1)}, u32[]{:S(2)}, u32[]{:S(2)}) %collective-permute-start) | collective-permute-done | bytes 524320 | tf_op jit(solution)/shard_map/ppermute | solution.py:403
  32.0 0.0 copy-done.4
  32.0 5.6 %shard_map.98 = (f32[32,4,128]{2,1,0:T(4,128)S(1)}, bf16[32,256,128]{2,1,0:T(8,128)(2,1)S(1)}) custom-call(s32[652]{0:T(1024)S(1)} %get-tuple-element.19.listed, s32[1]{0:T(128)} %get-tuple-element.20.total, bf16[8,256,128]{2,1,0:T(8,128)(2,1)S(1)} %all-to-all-done.mine, bf16[8,256,128]{2,1,0:T(8,128)(2,1)S(1)} %collective-permute-done.other, ...), custom_call_target="tpu_custom_call" | custom-call | flops 10000000000 | bytes 1000000 | tf_op jit(solution)/shard_map/pallas_call | solution.py:404
  37.6 21.5 %all_to_all.30.arrived = f32[32,4,128]{2,1,0:T(4,128)S(1)} all-to-all(f32[32,4,128]{2,1,0:T(4,128)S(1)} %get-tuple-element.24), channel_id=1, replica_groups=mesh['src_0'=4,'src_1'=8,'tgt_0'=8,'tgt_1'=2] {'src_0','src_1'}, dimensions={0} | all-to-all | bytes 131072 | tf_op jit(solution)/shard_map/all_to_all | solution.py:60
  59.2 0.1 shard_map.99
  59.2 12.0 %all_to_all.31.level = f32[32,4,128]{2,1,0:T(4,128)S(1)} all-to-all(f32[32,4,128]{2,1,0:T(4,128)S(1)} %shard_map.99), channel_id=1, replica_groups=mesh['src_0'=4,'src_1'=8,'tgt_0'=8,'tgt_1'=2] {'src_0','src_1'}, dimensions={0} | all-to-all | bytes 131072 | tf_op jit(solution)/shard_map/all_to_all | solution.py:60
  71.3 5.6 %shard_map.100 = f32[16,4,128]{2,1,0:T(4,128)} custom-call(s32[2]{0:T(128)S(1)} %pad_add_fusion.rank, s32[652]{0:T(1024)S(1)} %get-tuple-element.19.listed, s32[1]{0:T(128)} %get-tuple-element.20.total, bf16[32,256,128]{2,1,0:T(8,128)(2,1)S(1)} %get-tuple-element.23.x, bf16[64,16384]{1,0:T(8,128)(2,1)S(1)} %bitcast.10, f32[32,4,128]{2,1,0:T(4,128)S(1)} %all_to_all.31.level), custom_call_target="tpu_custom_call" | custom-call | flops 10000000000 | bytes 1000000 | tf_op jit(solution)/shard_map/pallas_call | solution.py:424
  76.9 8.1 %all-to-all-start.3 = ((f32[16,4,128]{2,1,0:T(4,128)}), f32[16,4,128]{2,1,0:T(4,128)S(1)}, u32[]{:S(2)}, u32[]{:S(2)}) async-start(f32[16,4,128]{2,1,0:T(4,128)} %shard_map.100), calls=%async_computation.3 | async-start | bytes 65536 | tf_op jit(solution)/shard_map/all_to_all | solution.py:60
  84.9 0.6 broadcast_multiply_fusion
  85.6 6.8 %all-to-all-done.3.arrived = f32[16,4,128]{2,1,0:T(4,128)S(1)} async-done(((f32[16,4,128]{2,1,0:T(4,128)}), f32[16,4,128]{2,1,0:T(4,128)S(1)}, u32[]{:S(2)}, u32[]{:S(2)}) %all-to-all-start.3) | async-done | bytes 32800 | tf_op jit(solution)/shard_map/all_to_all | solution.py:60
  92.4 0.6 shard_map.101
  93.0 9.8 %all_to_all.32.arrived = f32[16,1,128]{2,1,0:T(1,128)S(1)} all-to-all(f32[16,1,128]{2,1,0:T(1,128)S(1)} %get-tuple-element.28), channel_id=1, replica_groups=mesh['src_0'=4,'src_1'=8,'tgt_0'=8,'tgt_1'=2] {'tgt_0','tgt_1'}, dimensions={0} | all-to-all | bytes 16384 | tf_op jit(solution)/shard_map/all_to_all | solution.py:60
  102.9 12.7 %all_to_all.33.arrived = f32[32,1,128]{2,1,0:T(1,128)S(1)} all-to-all(f32[32,1,128]{2,1,0:T(1,128)S(1)} %shard_map.102), channel_id=1, replica_groups=mesh['src_0'=4,'src_1'=8,'tgt_0'=8,'tgt_1'=2] {'src_0','src_1'}, dimensions={0} | all-to-all | bytes 32768 | tf_op jit(solution)/shard_map/all_to_all | solution.py:60
  115.5 0.9 shard_map.103
  (3 shorter events, 0.0 us)
Async XLA Ops:
  0.6 0.8 copy-start.5
  1.5 8.7 %copy-start.6 = (s32[32,20]{0,1:T(8,128)S(1)}, s32[32,20]{0,1:T(8,128)}, u32[]{:S(2)}) copy-start(s32[32,20]{0,1:T(8,128)} %param.10) | copy-start | bytes 7684
  1.5 8.8 %copy-start = (f32[8,512]{1,0:T(8,128)S(1)}, f32[8,512]{1,0:T(8,128)}, u32[]{:S(2)}) copy-start(f32[8,512]{1,0:T(8,128)} %steps.1) | copy-start | bytes 49156
  1.5 8.8 %copy-start.1 = (f32[8,512]{1,0:T(8,128)S(1)}, f32[8,512]{1,0:T(8,128)}, u32[]{:S(2)}) copy-start(f32[8,512]{1,0:T(8,128)} %slopes.1) | copy-start | bytes 49156
  1.5 9.1 %copy-start.2 = (f32[8192]{0:T(1024)S(1)}, f32[8192]{0:T(1024)}, u32[]{:S(2)}) copy-start(f32[8192]{0:T(1024)} %param.9) | copy-start | bytes 98308
  1.5 9.8 %copy-start.3 = (s32[32]{0:T(128)S(1)}, s32[32]{0:T(128)}, u32[]{:S(2)}) copy-start(s32[32]{0:T(128)} %counts.1) | copy-start | bytes 388
  1.5 30.5 %copy-start.4 = (bf16[16384,64]{0,1:T(8,128)(2,1)S(1)}, bf16[16384,64]{0,1:T(8,128)(2,1)}, u32[]{:S(2)}) copy-start(bf16[16384,64]{0,1:T(8,128)(2,1)} %param.8) | copy-start | bytes 6291460
  2.5 22.4 %all-to-all-start = ((bf16[8,256,128]{2,1,0:T(8,128)(2,1)}), bf16[8,256,128]{2,1,0:T(8,128)(2,1)S(1)}, u32[]{:S(2)}, u32[]{:S(2)}) async-start(bf16[8,256,128]{2,1,0:T(8,128)(2,1)} %shard_map.94), calls=%async_computation | async-start | bytes 1048576 | tf_op jit(solution)/shard_map/all_to_all | solution.py:60
  24.9 7.1 %collective-permute-start = (bf16[8,256,128]{2,1,0:T(8,128)(2,1)S(1)}, bf16[8,256,128]{2,1,0:T(8,128)(2,1)S(1)}, u32[]{:S(2)}, u32[]{:S(2)}) collective-permute-start(bf16[8,256,128]{2,1,0:T(8,128)(2,1)S(1)} %all-to-all-done.mine), channel_id=1, source_target_pairs={{0,1},{1,0},{2,3},{3,2},{4,5},{5,4},{6,7},{7,6},{8,9},{9,8},{10,11... | collective-permute-start | bytes 1572872 | tf_op jit(solution)/shard_map/ppermute | solution.py:403
  76.9 15.6 %all-to-all-start.3 = ((f32[16,4,128]{2,1,0:T(4,128)}), f32[16,4,128]{2,1,0:T(4,128)S(1)}, u32[]{:S(2)}, u32[]{:S(2)}) async-start(f32[16,4,128]{2,1,0:T(4,128)} %shard_map.100), calls=%async_computation.3 | async-start | bytes 65536 | tf_op jit(solution)/shard_map/all_to_all | solution.py:60
